TPU v7x, 32 devices: a whole 2x2x4 slice. The times are simulated.
32 devices in a mesh: tok: 8 (over z, y), wid: 4 (over x, core).
Axes of the slice: x: 2, y: 2, z: 4, core: 2. Of those that a mesh axis runs over, the one named last changes fastest.
Arguments:
- g_inverse: bfloat16 [16384, 16384], P('tok', 'wid'), may hold values from -1 to 18, as said below
- a_inverse: bfloat16 [16384, 16384], P('tok', 'wid'), may hold values from -1 to 18, as said below
- query_out: bfloat16 [16384, 128], P(('tok', 'wid')), may hold values from -0.046875 to 0.046875
- query_in: bfloat16 [16384, 128], P(('tok', 'wid')), may hold values from -0.01171875 to 0.01171875
- output_grads: bfloat16 [16384, 16384], P('tok', 'wid'), may hold values from -6 to 6
- activations: bfloat16 [16384, 16384], P('tok', 'wid'), may hold values from -6 to 6
Outputs:
- scores: float32 [8, 16384], P(None, ('tok', 'wid'))
Inputs may be any that keep to these rules, and one draw needn't show every extreme that they name: g_inverse is symmetric. a_inverse is symmetric.
All inputs are finite; a program needn't handle non-finite values.
Results may differ from a plain program's by a relative error of at most 0.0041.
Values may be sent and summed in bfloat16 or wider, within the bound.
No kernel may reach another device: no remote copies, remote signals or barrier semaphores. Data moves between devices by JAX's collectives and lax.ppermute only.
A program may use at most 128 MiB of HBM per device.

v0:
```python
import jax
import jax.numpy as jnp
from jax import lax
from jax.sharding import PartitionSpec as P

QUERIES = 8
RANK = 16


def shards(g_inverse, a_inverse, query_out, query_in, output_grads, activations):
    column = lax.axis_index("wid")
    rows_out, rows_in = (
        lax.all_gather(query_out, "wid", axis=0, tiled=True),
        lax.all_gather(query_in, "wid", axis=0, tiled=True),
    )
    dims = (((0,), (0,)), ((), ()))
    part_out = lax.dot_general(g_inverse, rows_out, dims, preferred_element_type=jnp.float32)
    part_in = lax.dot_general(a_inverse, rows_in, dims, preferred_element_type=jnp.float32)
    sum_out, sum_in = lax.psum((part_out, part_in), "tok")
    g_pre = sum_out.astype(jnp.bfloat16)
    a_pre = sum_in.astype(jnp.bfloat16)
    out_part = jnp.dot(output_grads, g_pre, preferred_element_type=jnp.float32)
    in_part = jnp.dot(activations, a_pre, preferred_element_type=jnp.float32)
    share = output_grads.shape[0] // lax.axis_size("wid")
    total_out, total_in = lax.psum((out_part, in_part), "wid")
    out_proj = lax.dynamic_slice_in_dim(total_out, column * share, share, 0)
    in_proj = lax.dynamic_slice_in_dim(total_in, column * share, share, 0)
    product = out_proj * in_proj
    columns = product.shape[1]
    member = lax.broadcasted_iota(jnp.int32, (columns, QUERIES), 0) // RANK
    target = lax.broadcasted_iota(jnp.int32, (columns, QUERIES), 1)
    grouping = (member == target).astype(jnp.float32)
    return lax.dot_general(
        grouping,
        product,
        (((0,), (1,)), ((), ())),
        precision=lax.Precision.HIGHEST,
        preferred_element_type=jnp.float32,
    )


def solution(mesh):
    return jax.shard_map(
        shards,
        mesh=mesh,
        in_specs=(
            P("tok", "wid"),
            P("tok", "wid"),
            P(("tok", "wid"), None),
            P(("tok", "wid"), None),
            P("tok", "wid"),
            P("tok", "wid"),
        ),
        out_specs=P(None, ("tok", "wid")),
        check_vma=False,
    )
```

profile of v0, /device:TPU:0, one launch (start us, length us, event | category | flops | bytes accessed | tf_op | source)
XLA Modules:
  0.0 289.5 jit_solution(10388803165422396036)
XLA Ops:
  6.5 0.0 copy-start
  6.5 0.0 all-reduce.5.cloned.1.call-start
  6.5 0.0 copy-start.1
  6.5 8.9 %all_gather.7 = bf16[2048,128]{1,0:T(8,128)(2,1)S(1)} all-gather(bf16[512,128]{1,0:T(8,128)(2,1)} %param.9), channel_id=1, replica_groups=mesh['tok'=8,'wid'=4] {'wid'}, dimensions={0}, use_global_device_ids=true | all-gather | bytes 655360 | tf_op jit(solution)/shard_map/all_gather | solution.py:14
  15.5 8.2 %fusion.11 = f32[4096,128]{1,0:T(8,128)S(1)} fusion(bf16[2048,4096]{1,0:T(8,128)(2,1)} %param.7, bf16[2048,128]{1,0:T(8,128)(2,1)S(1)} %all_gather.7), kind=kOutput, calls=%fused_computation.19 | convolution fusion | flops 2147483648 | bytes 19398656 | tf_op jit(solution)/shard_map/dot_general | solution.py:18
  23.7 0.0 copy-done
  23.7 7.3 %all_gather.6 = bf16[2048,128]{1,0:T(8,128)(2,1)S(1)} all-gather(bf16[512,128]{1,0:T(8,128)(2,1)S(1)} %copy-done), channel_id=1, replica_groups=mesh['tok'=8,'wid'=4] {'wid'}, dimensions={0}, use_global_device_ids=true | all-gather | bytes 655360 | tf_op jit(solution)/shard_map/all_gather | solution.py:13
  31.0 0.0 copy-done.1
  31.0 6.2 %fusion.10 = f32[4096,128]{1,0:T(8,128)} fusion(bf16[2048,4096]{1,0:T(8,128)(2,1)S(1)} %copy-done.1, bf16[2048,128]{1,0:T(8,128)(2,1)S(1)} %all_gather.6), kind=kOutput, calls=%fused_computation.18 | convolution fusion | flops 2147483648 | bytes 19398656 | tf_op jit(solution)/shard_map/dot_general | solution.py:17
  37.2 168.2 %all-reduce.6 = (bf16[4096,128]{1,0:T(8,128)(2,1)}, bf16[4096,128]{1,0:T(8,128)(2,1)S(1)}) all-reduce(f32[4096,128]{1,0:T(8,128)S(1)} %fusion.11, f32[4096,128]{1,0:T(8,128)} %fusion.10), channel_id=1, replica_groups=mesh['tok'=8,'wid'=4] {'tok'}, use_global_device_ids=true, to_apply=%region_2.0 | all-reduce | flops 1048576 | bytes 6291456 | tf_op jit(solution)/shard_map/psum | solution.py:19
  205.3 12.8 %convolution_bitcast_fusion = f32[2048,128]{0,1:T(8,128)} fusion(bf16[2048,4096]{1,0:T(8,128)(2,1)} %param.11, bf16[4096,128]{1,0:T(8,128)(2,1)} %get-tuple-element.5), kind=kOutput, calls=%fused_computation | convolution fusion | flops 2147483648 | bytes 18874368 | tf_op jit(solution)/shard_map/dot_general | solution.py:23
  218.1 12.5 %convolution_bitcast_fusion.1 = f32[2048,128]{0,1:T(8,128)} fusion(bf16[2048,4096]{1,0:T(8,128)(2,1)} %param.10, bf16[4096,128]{1,0:T(8,128)(2,1)S(1)} %get-tuple-element.6), kind=kOutput, calls=%fused_computation.1 | convolution fusion | flops 2147483648 | bytes 18874368 | tf_op jit(solution)/shard_map/dot_general | solution.py:22
  230.6 0.0 all-reduce.5.cloned.1.call-update
  230.6 50.1 %all-reduce.5.cloned.1.call-done = (f32[2048,128]{0,1:T(8,128)}, f32[2048,128]{0,1:T(8,128)}) async-done(((f32[2048,128]{0,1:T(8,128)}, f32[2048,128]{0,1:T(8,128)}), (f32[2048,128]{0,1:T(8,128)}, f32[2048,128]{0,1:T(8,128)})) %all-reduce.5.cloned.1.call-update) | async-done | bytes 2097168 | tf_op jit(solution)/shard_map/psum | solution.py:25
  280.7 1.9 fusion.2
  (2 shorter events, 0.0 us)
Async XLA Ops:
  6.5 17.1 %copy-start = (bf16[512,128]{1,0:T(8,128)(2,1)S(1)}, bf16[512,128]{1,0:T(8,128)(2,1)}, u32[]{:S(2)}) copy-start(bf16[512,128]{1,0:T(8,128)(2,1)} %param.8) | copy-start | bytes 393220
  6.5 274.2 %all-reduce.5.cloned.1.call-start = ((), (), s32[]{:S(2)}) async-start(), calls=%async_computation | async-start | bytes 4194304 | tf_op jit(solution)/shard_map/psum | solution.py:25
  6.5 24.5 %copy-start.1 = (bf16[2048,4096]{1,0:T(8,128)(2,1)S(1)}, bf16[2048,4096]{1,0:T(8,128)(2,1)}, u32[]{:S(2)}) copy-start(bf16[2048,4096]{1,0:T(8,128)(2,1)} %param.6) | copy-start | bytes 50331652
Sparse Core Ops, SparseCore 0:
  230.7 49.9 all-reduce.4
where the time goes:
time: 290 us; the launch traced here: 289 us
  blocking collectives  184 us (63%)
  waiting for transfers between devices  50.1 us (17%)
  matrix products  41.6 us (14%)
  between operations  13.4 us (5%)
    psum x1, blocking collectives, shards(): sum_out, sum_in = lax.psum((part_out, part_in), 'tok')  168 us
    psum x1, waiting for transfers between devices, shards(): total_out, total_in = lax.psum((out_part, in_part), 'wid')  50.1 us
    dot_general x1, matrix products, shards(): in_part = jnp.dot(activations, a_pre, preferred_element_type=jnp.float32)  12.8 us
    dot_general x1, matrix products, shards(): out_part = jnp.dot(output_grads, g_pre, preferred_element_type=jnp.float32)  12.5 us
    all_gather x1, blocking collectives, shards(): lax.all_gather(query_in, 'wid', axis=0, tiled=True)  8.95 us
    dot_general x1, matrix products, shards(): lax.dot_general(a_inverse, rows_in, dims, preferred_element_type=jnp.floa...  8.19 us
    all_gather x1, blocking collectives, shards(): lax.all_gather(query_out, 'wid', axis=0, tiled=True)  7.3 us
    dot_general x1, matrix products, shards(): lax.dot_general(g_inverse, rows_out, dims, preferred_element_type=jnp.flo...  6.16 us
  transfers between devices with their start and end apart: 1, of which 1 were waited for; matrix products, arithmetic and copies ran while one was open for 0% of the time, Pallas kernels for 0%

commit v1 on v0

v1 whole, which is shorter than its diff:
```python
import functools

import jax
import jax.numpy as jnp
import numpy as np
from jax import lax
from jax.experimental import pallas as pl
from jax.experimental.pallas import tpu as pltpu
from jax.sharding import PartitionSpec as P

QUERIES = 8
RANK = 16
LANES = 128
F32 = jnp.float32
BF16 = jnp.bfloat16
GRANT = 4 << 20
COST = 2
VMEM = pl.BlockSpec(memory_space=pltpu.VMEM)
SMEM = pl.BlockSpec(memory_space=pltpu.SMEM)
HBM = pl.BlockSpec(memory_space=pltpu.HBM)
WIRE_G = F32
WIRE_A = BF16
HOLD = 30 * 10**6
ANY = pl.BlockSpec(memory_space=pl.ANY)


def ring_order(size):
    rows = 1
    while rows * rows < size:
        rows *= 2
    cols = size // rows
    if rows * cols != size or cols < 2:
        return list(range(size))
    cycle = [(r, 0) for r in range(rows)]
    for i, r in enumerate(reversed(range(rows))):
        walk = range(1, cols) if i % 2 == 0 else range(cols - 1, 0, -1)
        cycle += [(r, c) for c in walk]
    return [r * cols + c for r, c in cycle]


def reversed_bits(j, bits):
    return sum(((j >> b) & 1) << (bits - 1 - b) for b in range(bits))


def gate_body(small, *refs):
    refs[-1][...] = small[...]


def gate(small, cost, after=()):
    return pl.pallas_call(
        gate_body,
        in_specs=[VMEM] + [ANY] * len(after),
        out_specs=VMEM,
        out_shape=jax.ShapeDtypeStruct(small.shape, small.dtype),
        compiler_params=pltpu.CompilerParams(vmem_limit_bytes=GRANT),
        cost_estimate=pl.CostEstimate(flops=0, bytes_accessed=cost, transcendentals=0),
    )(small, *after)


def turn_body(base, ids, *refs):
    queries, out = refs[:-1], refs[-1]
    height = queries[0].shape[0]
    for k, query in enumerate(queries):
        out[:, pl.ds(pl.multiple_of(ids[base + k] * height, height), height)] = query[...].T


def turn(ids, base, queries):
    return pl.pallas_call(
        functools.partial(turn_body, base),
        in_specs=[SMEM] + [VMEM] * len(queries),
        out_specs=VMEM,
        out_shape=jax.ShapeDtypeStruct((LANES, len(queries) * queries[0].shape[0]), BF16),
        compiler_params=pltpu.CompilerParams(vmem_limit_bytes=GRANT),
    )(ids, *queries)


def partials_body(columns, ids, turned, inverse, *refs):
    outs = refs[-len(columns) :]
    width = outs[0].shape[0]
    for column, out in zip(columns, outs):
        block = inverse[:, pl.ds(pl.multiple_of(ids[column] * width, width), width)]
        out[...] = jnp.dot(turned[...], block, preferred_element_type=F32).T


def partials(ids, turned, inverse, columns, width, after):
    n = len(columns)
    return pl.pallas_call(
        functools.partial(partials_body, columns),
        in_specs=[SMEM, VMEM, VMEM] + [ANY] * len(after),
        out_specs=[VMEM] * n,
        out_shape=[jax.ShapeDtypeStruct((width, LANES), F32)] * n,
        compiler_params=pltpu.CompilerParams(vmem_limit_bytes=GRANT),
        cost_estimate=pl.CostEstimate(
            flops=2 * n * width * turned.size,
            bytes_accessed=COST * n * width * inverse.shape[0],
            transcendentals=0,
        ),
    )(ids, turned, inverse, *after)


def project_body(columns, first, tile, count, ids, *refs):
    n, tokens, out = len(columns), refs[-2], refs[-1]
    factors, total = refs[:n], None if first else refs[n]
    height = tokens.shape[0] // count
    for j in range(count):
        rows = slice(j * height, (j + 1) * height)
        here = pl.ds(pl.multiple_of(ids[tile + j] * height, height), height)
        acc = None if first else total[rows, :]
        for column, factor in zip(columns, factors):
            width = factor.shape[0]
            block = tokens[here, pl.ds(pl.multiple_of(ids[column] * width, width), width)]
            term = jnp.dot(block, factor[...], preferred_element_type=F32)
            acc = term if acc is None else acc + term
        out[rows, :] = acc


def project(ids, columns, factors, total, tokens, tile, count):
    n, first = len(factors), total is None
    rows, width = tokens.shape[0], factors[0].shape[0]
    return pl.pallas_call(
        functools.partial(project_body, columns, first, tile, count),
        in_specs=[SMEM] + [VMEM] * (n + (not first) + 1),
        out_specs=VMEM,
        out_shape=jax.ShapeDtypeStruct((rows, LANES), F32),
        compiler_params=pltpu.CompilerParams(vmem_limit_bytes=GRANT),
        cost_estimate=pl.CostEstimate(
            flops=2 * n * rows * width * LANES,
            bytes_accessed=COST * n * rows * width,
            transcendentals=0,
        ),
    )(ids, *factors, *([] if first else [total]), tokens)


def score_body(out_ref, in_ref, arrived_ref, scores_ref):
    product = out_ref[...] * (in_ref[...] + arrived_ref[...].astype(F32))
    scores_ref[...] = product.T.reshape(QUERIES, RANK, product.shape[0]).sum(axis=1)


def score(out_proj, in_proj, arrived):
    rows = out_proj.shape[0]
    return pl.pallas_call(score_body, out_shape=jax.ShapeDtypeStruct((QUERIES, rows), F32))(
        out_proj, in_proj, arrived
    )


def program(tok, wid, g_inverse, a_inverse, query_out, query_in, output_grads, activations):
    bits = wid.bit_length() - 1
    cycle = ring_order(tok)
    width = g_inverse.shape[1] // tok
    height = g_inverse.shape[0] // wid
    share = output_grads.shape[0] // wid
    ahead, behind = tok // 2, (tok - 1) // 2
    sides = max(ahead, behind + 1)
    kernels = width % LANES == 0 and height % LANES == 0 and share % LANES == 0

    row_at, tile_at = tok, tok + wid
    table = np.zeros((tok, wid, tok + 2 * wid), np.int32)
    for t in range(tok):
        for w in range(wid):
            table[t, w, :tok] = (cycle.index(t) + np.arange(tok)) % tok
            table[t, w, row_at:tile_at] = w ^ np.arange(wid)
            table[t, w, tile_at:] = [w ^ reversed_bits(j, bits) for j in range(wid)]
    ids = jnp.asarray(table)[lax.axis_index("tok"), lax.axis_index("wid")]

    def shift(x, step):
        return lax.ppermute(x, "tok", [(cycle[i], cycle[(i + step) % tok]) for i in range(tok)])

    def swap(x, mask):
        return lax.ppermute(x, "wid", [(w, w ^ mask) for w in range(wid)])

    def at(offset):
        return offset % tok

    def gather_query(query):
        return [query] + [swap(query, k) for k in range(1, wid)]

    def make_partials(inverse, queries, columns):
        outs = []
        for column in columns:
            cut = lax.dynamic_slice_in_dim(inverse, ids[column] * width, width, 1)
            total = 0
            for k, query in enumerate(queries):
                block = lax.dynamic_slice_in_dim(cut, ids[row_at + k] * height, height, 0)
                total += lax.dot_general(block, query, (((0,), (0,)), ((), ())), preferred_element_type=F32)
            outs.append(total)
        return outs

    def make_project(tokens, columns, factors, total):
        outs = []
        for j in range(wid):
            cut = lax.dynamic_slice_in_dim(tokens, ids[tile_at + j] * share, share, 0)
            part = 0 if total is None else total[j * share : (j + 1) * share]
            for factor, column in zip(factors, columns):
                block = lax.dynamic_slice_in_dim(cut, ids[column] * width, width, 1)
                part += jnp.dot(block, factor, preferred_element_type=F32)
            outs.append(part)
        return jnp.concatenate(outs, axis=0)

    def precondition(inverse, queries, way, wire, after):
        turned = turn(ids, row_at, queries) if kernels else queries
        first = None
        for k in range(sides + 1):
            if k == 1:
                front, back = fwd.astype(wire), bwd.astype(wire)
            if 1 <= k <= ahead:
                last, front = front, shift(front, way)
            if 1 <= k <= behind:
                back = shift(back, -way)
            if k < sides:
                columns = [at(way * (ahead - k)), at(way * (k - behind))]
                if kernels:
                    fwd, bwd = partials(ids, turned, inverse, columns, width, after if k == 0 else [last])
                else:
                    fwd, bwd = make_partials(inverse, queries, columns)
                last = first = fwd if k == 0 else first
            if 1 <= k < ahead:
                front = (front.astype(F32) + fwd).astype(wire)
            if 1 <= k < behind:
                back = (back.astype(F32) + bwd).astype(wire)
        return (front.astype(F32) + back.astype(F32) + bwd).astype(BF16), first

    def gather_project(tokens, factor, way, cuts):
        front = back = factor
        total = None
        factors, columns = [factor], [at(0)]
        for k in range(1, ahead + 1):
            front = shift(front, way)
            factors.append(front)
            columns.append(at(-way * k))
            if k <= behind:
                back = shift(back, -way)
                factors.append(back)
                columns.append(at(way * k))
            if k in cuts or k == ahead:
                if kernels:
                    total = project(ids, columns, factors, total, tokens, tile_at, wid)
                else:
                    total = make_project(tokens, columns, factors, total)
                factors, columns = [], []
        return total

    def scatter(total, last):
        for b in range(bits):
            half = total.shape[0] // 2
            arrived = swap(total[half:], 1 << b)
            if b == bits - 1 and not last:
                return total[:half], arrived
            total = total[:half] + arrived
        return total

    q_in = gather_query(query_in)
    if kernels:
        query_out = gate(query_out, HOLD)
    q_out = gather_query(query_out)
    a_pre, first = precondition(a_inverse, q_in, 1, WIRE_A, [])
    g_pre, _ = precondition(g_inverse, q_out, -1, WIRE_G, [first])
    in_proj = scatter(gather_project(activations, a_pre, 1, ()), True)
    out_proj, arrived = scatter(gather_project(output_grads, g_pre, -1, (2,)), False)
    return score(in_proj, out_proj, arrived)


def solution(mesh):
    return jax.shard_map(
        functools.partial(program, mesh.shape["tok"], mesh.shape["wid"]),
        mesh=mesh,
        in_specs=(
            P("tok", "wid"),
            P("tok", "wid"),
            P(("tok", "wid"), None),
            P(("tok", "wid"), None),
            P("tok", "wid"),
            P("tok", "wid"),
        ),
        out_specs=P(None, ("tok", "wid")),
        check_vma=False,
    )
```

time: 290 us -> 120 us (0.41)
  blocking collectives: 184 us -> 0 us
  matrix products: 41.6 us -> 0 us
  starting transfers between devices: 0.01 us -> 36.2 us
  Pallas kernels: 0 us -> 25.1 us
  local copies, waits for them, and re-layouts: 0.01 us -> 23.5 us
  waiting for transfers between devices: 50.1 us -> 33 us
  between operations: 13.4 us -> 0.36 us
    psum x1 -> x0, blocking collectives: 168 us -> none  [shards(): sum_out, sum_in = lax.psum((part_out, part_in), 'tok')]
    psum x1 -> x0, waiting for transfers between devices: 50.1 us -> none  [shards(): total_out, total_in = lax.psum((out_part, in_part), 'wid')]
    dot_general x5 -> x0, matrix products: 41.6 us -> none  [the longest x1 12.8 us: shards(): in_part = jnp.dot(activations, a_pre, preferred_element_type=jnp.float32)]
    ppermute x0 -> x38, starting transfers between devices: none -> 36.2 us  [the longest x28 27.9 us: shift(): lax.ppermute(x, 'tok', [(cycle[i], cycle[(i + step) % tok]) for i in rang...]
    ppermute x0 -> x38, waiting for transfers between devices: none -> 33 us  [the longest x28 20 us: shift(): lax.ppermute(x, 'tok', [(cycle[i], cycle[(i + step) % tok]) for i in rang...]
    pallas_call x0 -> x15, Pallas kernels: none -> 25.1 us  [the longest x8 11 us: partials(): pl.pallas_call(functools.partial(partials_body, columns), in_specs=[SMEM,...]
    unnamed x4 -> x30, local copies, waits for them, and re-layouts: 0.01 us -> 22 us
    all_gather x2 -> x0, blocking collectives: 16.2 us -> none  [the longest x1 8.95 us: shards(): lax.all_gather(query_in, 'wid', axis=0, tiled=True)]
  transfers between devices with their start and end apart: 1 -> 38, of which waited for: 1 -> 18; matrix products, arithmetic and copies ran while one was open for 0% -> 2% of each run, Pallas kernels for 0% -> 19%
where the time goes in v1:
time: 120 us; the launch traced here: 119 us
  starting transfers between devices  36.2 us (30%)
  waiting for transfers between devices  33 us (28%)
  Pallas kernels  25.1 us (21%)
  local copies, waits for them, and re-layouts  23.5 us (20%)
  other arithmetic  1.25 us (1%)
    ppermute x28, starting transfers between devices, shift(): lax.ppermute(x, 'tok', [(cycle[i], cycle[(i + step) % tok]) for i in rang...  27.9 us
    unnamed x30, local copies, waits for them, and re-layouts  22 us
    ppermute x28, waiting for transfers between devices, shift(): lax.ppermute(x, 'tok', [(cycle[i], cycle[(i + step) % tok]) for i in rang...  20 us
    ppermute x10, waiting for transfers between devices, swap(): return lax.ppermute(x, 'wid', [(w, w ^ mask) for w in range(wid)])  13 us
    pallas_call x8, Pallas kernels, partials(): pl.pallas_call(functools.partial(partials_body, columns), in_specs=[SMEM,...  11 us
    pallas_call x3, Pallas kernels, project(): pl.pallas_call(functools.partial(project_body, columns, first, tile, coun...  10.7 us
    ppermute x10, starting transfers between devices, swap(): return lax.ppermute(x, 'wid', [(w, w ^ mask) for w in range(wid)])  8.33 us
  transfers between devices with their start and end apart: 38, of which 18 were waited for; matrix products, arithmetic and copies ran while one was open for 2% of the time, Pallas kernels for 19%

profile of v1, /device:TPU:0, one launch (start us, length us, event | category | flops | bytes accessed | tf_op | source)
XLA Modules:
  0.0 119.5 jit_solution(10397107502869310761)
XLA Ops:
  0.5 2.5 %collective-permute-start.1 = (bf16[512,128]{1,0:T(8,128)(2,1)}, bf16[512,128]{1,0:T(8,128)(2,1)S(1)}, u32[]{:S(2)}, u32[]{:S(2)}) collective-permute-start(bf16[512,128]{1,0:T(8,128)(2,1)} %refs_0_.1), channel_id=1, source_target_pairs={{0,2},{1,3},{2,0},{3,1},{4,6},{5,7},{6,4},{7,5},{8,10},{9,11},{10,... | collective-permute-start | bytes 393224 | tf_op jit(solution)/shard_map/ppermute | solution.py:169
  3.1 0.9 copy-done.4
  4.2 1.9 %collective-permute-start.20 = (bf16[512,128]{1,0:T(8,128)(2,1)S(1)}, bf16[512,128]{1,0:T(8,128)(2,1)S(1)}, u32[]{:S(2)}, u32[]{:S(2)}) collective-permute-start(bf16[512,128]{1,0:T(8,128)(2,1)S(1)} %shard_map.79.refs_0_), channel_id=1, source_target_pairs={{0,2},{1,3},{2,0},{3,1},{4,6},{5,7},{6,4},{7,5},{8,10},{9,11},{10,... | collective-permute-start | bytes 393224 | tf_op jit(solution)/shard_map/ppermute | solution.py:169
  6.1 0.7 dynamic-slice_bitcast_fusion.ids
  6.8 0.7 collective-permute-done.1.refs_2_
  7.5 2.4 %collective-permute-done.2.refs_3_ = bf16[512,128]{1,0:T(8,128)(2,1)S(1)} collective-permute-done((bf16[512,128]{1,0:T(8,128)(2,1)}, bf16[512,128]{1,0:T(8,128)(2,1)S(1)}, u32[]{:S(2)}, u32[]{:S(2)}) %collective-permute-start.2) | collective-permute-done | bytes 131104 | tf_op jit(solution)/shard_map/ppermute | solution.py:169
  9.9 0.9 copy-done.5
  10.8 0.7 shard_map.73.turned
  11.6 5.8 %copy-done = bf16[2048,4096]{1,0:T(8,128)(2,1)S(1)} copy-done((bf16[2048,4096]{1,0:T(8,128)(2,1)S(1)}, bf16[2048,4096]{1,0:T(8,128)(2,1)}, u32[]{:S(2)}) %copy-start) | copy-done | bytes 16777240
  17.4 1.4 %shard_map.74 = (f32[512,128]{1,0:T(8,128)S(1)}, f32[512,128]{1,0:T(8,128)S(1)}) custom-call(s32[16]{0:T(128)S(1)} %dynamic-slice_bitcast_fusion.ids, bf16[128,2048]{1,0:T(8,128)(2,1)S(1)} %shard_map.73.turned, bf16[2048,4096]{1,0:T(8,128)(2,1)S(1)} %copy-done), custom_call_target="tpu_custom_call" | custom-call | flops 536870912 | bytes 4194304 | tf_op jit(solution)/shard_map/pallas_call | solution.py:87
  18.8 1.7 %collective-permute-start.3 = (bf16[512,128]{1,0:T(8,128)(2,1)S(1)}, bf16[512,128]{1,0:T(8,128)(2,1)S(1)}, u32[]{:S(2)}, u32[]{:S(2)}) collective-permute-start(bf16[512,128]{1,0:T(8,128)(2,1)S(1)} %convert_element_type.48.refs_0_), channel_id=1, source_target_pairs={{0,8},{8,16},{16,24},{24,28},{28,20},{20,12},{12,4},{4,0},{1,9},{9... | collective-permute-start | bytes 393224 | tf_op jit(solution)/shard_map/ppermute | solution.py:166
  20.9 0.7 shard_map.80.turned
  21.7 5.8 %copy-done.1 = bf16[2048,4096]{1,0:T(8,128)(2,1)S(1)} copy-done((bf16[2048,4096]{1,0:T(8,128)(2,1)S(1)}, bf16[2048,4096]{1,0:T(8,128)(2,1)}, u32[]{:S(2)}) %copy-start.1) | copy-done | bytes 16777240
  27.4 1.4 %shard_map.81 = (f32[512,128]{1,0:T(8,128)S(1)}, f32[512,128]{1,0:T(8,128)S(1)}) custom-call(s32[16]{0:T(128)S(1)} %dynamic-slice_bitcast_fusion.ids, bf16[128,2048]{1,0:T(8,128)(2,1)S(1)} %shard_map.80.turned, bf16[2048,4096]{1,0:T(8,128)(2,1)S(1)} %copy-done.1, f32[512,128]{1,0:T(8,128)S(1)} %get-tuple-element.21.refs_0_), custom_call_target="tpu_custom_call" | custom-call | flops 536870912 | bytes 4194304 | tf_op jit(solution)/shard_map/pallas_call | solution.py:87
  28.8 1.6 %collective-permute-start.22 = (f32[512,128]{1,0:T(8,128)S(1)}, f32[512,128]{1,0:T(8,128)S(1)}, u32[]{:S(2)}, u32[]{:S(2)}) collective-permute-start(f32[512,128]{1,0:T(8,128)S(1)} %get-tuple-element.29.refs_0_), channel_id=1, source_target_pairs={{0,4},{8,0},{16,8},{24,16},{28,24},{20,28},{12,20},{4,12},{1,5},{9... | collective-permute-start | bytes 786440 | tf_op jit(solution)/shard_map/ppermute | solution.py:166
  30.4 0.5 collective-permute-start.26
  30.9 1.4 %shard_map.75 = (f32[512,128]{1,0:T(8,128)S(1)}, f32[512,128]{1,0:T(8,128)S(1)}) custom-call(s32[16]{0:T(128)S(1)} %dynamic-slice_bitcast_fusion.ids, bf16[128,2048]{1,0:T(8,128)(2,1)S(1)} %shard_map.73.turned, bf16[2048,4096]{1,0:T(8,128)(2,1)S(1)} %bitcast.3, bf16[512,128]{1,0:T(8,128)(2,1)S(1)} %convert_element_type.48.refs_0_), custom_call_target="tpu_custom_call" | custom-call | flops 536870912 | bytes 4194304 | tf_op jit(solution)/shard_map/pallas_call | solution.py:87
  32.3 2.2 %copy-done.2 = bf16[2048,4096]{1,0:T(8,128)(2,1)S(1)} copy-done((bf16[2048,4096]{1,0:T(8,128)(2,1)S(1)}, bf16[2048,4096]{1,0:T(8,128)(2,1)}, u32[]{:S(2)}) %copy-start.2) | copy-done | bytes 16777240
  34.5 1.4 %shard_map.82 = (f32[512,128]{1,0:T(8,128)S(1)}, f32[512,128]{1,0:T(8,128)S(1)}) custom-call(s32[16]{0:T(128)S(1)} %dynamic-slice_bitcast_fusion.ids, bf16[128,2048]{1,0:T(8,128)(2,1)S(1)} %shard_map.80.turned, bf16[2048,4096]{1,0:T(8,128)(2,1)S(1)} %copy-done.2, f32[512,128]{1,0:T(8,128)S(1)} %get-tuple-element.29.refs_0_), custom_call_target="tpu_custom_call" | custom-call | flops 536870912 | bytes 4194304 | tf_op jit(solution)/shard_map/pallas_call | solution.py:87
  35.9 1.7 %collective-permute-start.4 = (bf16[512,128]{1,0:T(8,128)(2,1)S(1)}, bf16[512,128]{1,0:T(8,128)(2,1)S(1)}, u32[]{:S(2)}, u32[]{:S(2)}) collective-permute-start(bf16[512,128]{1,0:T(8,128)(2,1)S(1)} %add_convert_fusion.6.refs_0_), channel_id=1, source_target_pairs={{0,8},{8,16},{16,24},{24,28},{28,20},{20,12},{12,4},{4,0},{1,9},{9... | collective-permute-start | bytes 393224 | tf_op jit(solution)/shard_map/ppermute | solution.py:166
  37.6 1.4 %shard_map.76 = (f32[512,128]{1,0:T(8,128)S(1)}, f32[512,128]{1,0:T(8,128)S(1)}) custom-call(s32[16]{0:T(128)S(1)} %dynamic-slice_bitcast_fusion.ids, bf16[128,2048]{1,0:T(8,128)(2,1)S(1)} %shard_map.73.turned, bf16[2048,4096]{1,0:T(8,128)(2,1)S(1)} %bitcast.3, bf16[512,128]{1,0:T(8,128)(2,1)S(1)} %add_convert_fusion.6.refs_0_), custom_call_target="tpu_custom_call" | custom-call | flops 536870912 | bytes 4194304 | tf_op jit(solution)/shard_map/pallas_call | solution.py:87
  39.0 0.5 collective-permute-start.8
  39.5 2.1 %collective-permute-done.4 = bf16[512,128]{1,0:T(8,128)(2,1)S(1)} collective-permute-done((bf16[512,128]{1,0:T(8,128)(2,1)S(1)}, bf16[512,128]{1,0:T(8,128)(2,1)S(1)}, u32[]{:S(2)}, u32[]{:S(2)}) %collective-permute-start.4) | collective-permute-done | bytes 131104 | tf_op jit(solution)/shard_map/ppermute | solution.py:166
  41.6 1.7 %collective-permute-start.5 = (bf16[512,128]{1,0:T(8,128)(2,1)S(1)}, bf16[512,128]{1,0:T(8,128)(2,1)S(1)}, u32[]{:S(2)}, u32[]{:S(2)}) collective-permute-start(bf16[512,128]{1,0:T(8,128)(2,1)S(1)} %add_convert_fusion.5.refs_0_), channel_id=1, source_target_pairs={{0,8},{8,16},{16,24},{24,28},{28,20},{20,12},{12,4},{4,0},{1,9},{9... | collective-permute-start | bytes 393224 | tf_op jit(solution)/shard_map/ppermute | solution.py:166
  43.8 0.7 collective-permute-done.8
  44.5 0.8 collective-permute-start.9
  45.3 1.4 %collective-permute-start.27 = (f32[512,128]{1,0:T(8,128)S(1)}, f32[512,128]{1,0:T(8,128)S(1)}, u32[]{:S(2)}, u32[]{:S(2)}) collective-permute-start(f32[512,128]{1,0:T(8,128)S(1)} %add.71), channel_id=1, source_target_pairs={{0,8},{8,16},{16,24},{24,28},{28,20},{20,12},{12,4},{4,0},{1,9},{9... | collective-permute-start | bytes 786440 | tf_op jit(solution)/shard_map/ppermute | solution.py:166
  46.7 1.4 %shard_map.77 = (f32[512,128]{1,0:T(8,128)S(1)}, f32[512,128]{1,0:T(8,128)S(1)}) custom-call(s32[16]{0:T(128)S(1)} %dynamic-slice_bitcast_fusion.ids, bf16[128,2048]{1,0:T(8,128)(2,1)S(1)} %shard_map.73.turned, bf16[2048,4096]{1,0:T(8,128)(2,1)S(1)} %bitcast.3, bf16[512,128]{1,0:T(8,128)(2,1)S(1)} %add_convert_fusion.5.refs_0_), custom_call_target="tpu_custom_call" | custom-call | flops 536870912 | bytes 4194304 | tf_op jit(solution)/shard_map/pallas_call | solution.py:87
  48.0 1.4 %shard_map.83 = (f32[512,128]{1,0:T(8,128)S(1)}, f32[512,128]{1,0:T(8,128)S(1)}) custom-call(s32[16]{0:T(128)S(1)} %dynamic-slice_bitcast_fusion.ids, bf16[128,2048]{1,0:T(8,128)(2,1)S(1)} %shard_map.80.turned, bf16[2048,4096]{1,0:T(8,128)(2,1)S(1)} %copy-done.2, f32[512,128]{1,0:T(8,128)S(1)} %add.68.refs_0_), custom_call_target="tpu_custom_call" | custom-call | flops 536870912 | bytes 4194304 | tf_op jit(solution)/shard_map/pallas_call | solution.py:87
  49.4 3.3 %collective-permute-done.23 = f32[512,128]{1,0:T(8,128)S(1)} collective-permute-done((f32[512,128]{1,0:T(8,128)S(1)}, f32[512,128]{1,0:T(8,128)S(1)}, u32[]{:S(2)}, u32[]{:S(2)}) %collective-permute-start.23) | collective-permute-done | bytes 262176 | tf_op jit(solution)/shard_map/ppermute | solution.py:166
  53.0 1.8 %collective-permute-start.6 = (bf16[512,128]{1,0:T(8,128)(2,1)S(1)}, bf16[512,128]{1,0:T(8,128)(2,1)S(1)}, u32[]{:S(2)}, u32[]{:S(2)}) collective-permute-start(bf16[512,128]{1,0:T(8,128)(2,1)S(1)} %add_convert_fusion.4), channel_id=1, source_target_pairs={{0,8},{8,16},{16,24},{24,28},{28,20},{20,12},{12,4},{4,0},{1,9},{9... | collective-permute-start | bytes 393224 | tf_op jit(solution)/shard_map/ppermute | solution.py:166
  54.9 1.6 %collective-permute-start.28 = (f32[512,128]{1,0:T(8,128)S(1)}, f32[512,128]{1,0:T(8,128)S(1)}, u32[]{:S(2)}, u32[]{:S(2)}) collective-permute-start(f32[512,128]{1,0:T(8,128)S(1)} %add.72), channel_id=1, source_target_pairs={{0,8},{8,16},{16,24},{24,28},{28,20},{20,12},{12,4},{4,0},{1,9},{9... | collective-permute-start | bytes 786440 | tf_op jit(solution)/shard_map/ppermute | solution.py:166
  56.5 1.4 %shard_map.84 = (f32[512,128]{1,0:T(8,128)S(1)}, f32[512,128]{1,0:T(8,128)S(1)}) custom-call(s32[16]{0:T(128)S(1)} %dynamic-slice_bitcast_fusion.ids, bf16[128,2048]{1,0:T(8,128)(2,1)S(1)} %shard_map.80.turned, bf16[2048,4096]{1,0:T(8,128)(2,1)S(1)} %copy-done.2, f32[512,128]{1,0:T(8,128)S(1)} %add.69.refs_0_), custom_call_target="tpu_custom_call" | custom-call | flops 536870912 | bytes 4194304 | tf_op jit(solution)/shard_map/pallas_call | solution.py:87
  57.9 1.3 %collective-permute-done.24 = f32[512,128]{1,0:T(8,128)S(1)} collective-permute-done((f32[512,128]{1,0:T(8,128)S(1)}, f32[512,128]{1,0:T(8,128)S(1)}, u32[]{:S(2)}, u32[]{:S(2)}) %collective-permute-start.24) | collective-permute-done | bytes 262176 | tf_op jit(solution)/shard_map/ppermute | solution.py:166
  59.7 1.8 %collective-permute-start.10 = (bf16[512,128]{1,0:T(8,128)(2,1)S(1)}, bf16[512,128]{1,0:T(8,128)(2,1)S(1)}, u32[]{:S(2)}, u32[]{:S(2)}) collective-permute-start(bf16[512,128]{1,0:T(8,128)(2,1)S(1)} %add_convert_fusion.1.refs_0_), channel_id=1, source_target_pairs={{0,8},{8,16},{16,24},{24,28},{28,20},{20,12},{12,4},{4,0},{1,9},{9... | collective-permute-start | bytes 393224 | tf_op jit(solution)/shard_map/ppermute | solution.py:166
  61.8 2.9 %collective-permute-done.10.refs_1_ = bf16[512,128]{1,0:T(8,128)(2,1)S(1)} collective-permute-done((bf16[512,128]{1,0:T(8,128)(2,1)S(1)}, bf16[512,128]{1,0:T(8,128)(2,1)S(1)}, u32[]{:S(2)}, u32[]{:S(2)}) %collective-permute-start.10) | collective-permute-done | bytes 131104 | tf_op jit(solution)/shard_map/ppermute | solution.py:166
  64.7 1.7 %collective-permute-start.12 = (bf16[512,128]{1,0:T(8,128)(2,1)S(1)}, bf16[512,128]{1,0:T(8,128)(2,1)S(1)}, u32[]{:S(2)}, u32[]{:S(2)}) collective-permute-start(bf16[512,128]{1,0:T(8,128)(2,1)S(1)} %collective-permute-done.10.refs_1_), channel_id=1, source_target_pairs={{0,8},{8,16},{16,24},{24,28},{28,20},{20,12},{12,4},{4,0},{1,9},{9... | collective-permute-start | bytes 393224 | tf_op jit(solution)/shard_map/ppermute | solution.py:166
  66.5 0.7 collective-permute-start.29
  67.2 1.6 %collective-permute-done.11.refs_2_ = bf16[512,128]{1,0:T(8,128)(2,1)S(1)} collective-permute-done((bf16[512,128]{1,0:T(8,128)(2,1)S(1)}, bf16[512,128]{1,0:T(8,128)(2,1)S(1)}, u32[]{:S(2)}, u32[]{:S(2)}) %collective-permute-start.11) | collective-permute-done | bytes 131104 | tf_op jit(solution)/shard_map/ppermute | solution.py:166
  69.2 1.8 %collective-permute-done.12.refs_3_ = bf16[512,128]{1,0:T(8,128)(2,1)S(1)} collective-permute-done((bf16[512,128]{1,0:T(8,128)(2,1)S(1)}, bf16[512,128]{1,0:T(8,128)(2,1)S(1)}, u32[]{:S(2)}, u32[]{:S(2)}) %collective-permute-start.12) | collective-permute-done | bytes 131104 | tf_op jit(solution)/shard_map/ppermute | solution.py:166
  71.0 1.1 collective-permute-start.14
  72.1 1.7 %collective-permute-start.32 = (bf16[512,128]{1,0:T(8,128)(2,1)S(1)}, bf16[512,128]{1,0:T(8,128)(2,1)S(1)}, u32[]{:S(2)}, u32[]{:S(2)}) collective-permute-start(bf16[512,128]{1,0:T(8,128)(2,1)S(1)} %add_convert_fusion.refs_0_), channel_id=1, source_target_pairs={{0,8},{8,16},{16,24},{24,28},{28,20},{20,12},{12,4},{4,0},{1,9},{9... | collective-permute-start | bytes 393224 | tf_op jit(solution)/shard_map/ppermute | solution.py:166
  74.1 1.0 collective-permute-done.13.refs_4_
  75.5 2.2 %collective-permute-done.14.refs_5_ = bf16[512,128]{1,0:T(8,128)(2,1)S(1)} collective-permute-done((bf16[512,128]{1,0:T(8,128)(2,1)S(1)}, bf16[512,128]{1,0:T(8,128)(2,1)S(1)}, u32[]{:S(2)}, u32[]{:S(2)}) %collective-permute-start.14) | collective-permute-done | bytes 131104 | tf_op jit(solution)/shard_map/ppermute | solution.py:166
  77.7 0.7 collective-permute-start.16
  78.5 1.4 %collective-permute-done.32.refs_2_ = bf16[512,128]{1,0:T(8,128)(2,1)S(1)} collective-permute-done((bf16[512,128]{1,0:T(8,128)(2,1)S(1)}, bf16[512,128]{1,0:T(8,128)(2,1)S(1)}, u32[]{:S(2)}, u32[]{:S(2)}) %collective-permute-start.32) | collective-permute-done | bytes 131104 | tf_op jit(solution)/shard_map/ppermute | solution.py:166
  79.9 1.3 %collective-permute-start.33 = (bf16[512,128]{1,0:T(8,128)(2,1)S(1)}, bf16[512,128]{1,0:T(8,128)(2,1)S(1)}, u32[]{:S(2)}, u32[]{:S(2)}) collective-permute-start(bf16[512,128]{1,0:T(8,128)(2,1)S(1)} %collective-permute-done.32.refs_2_), channel_id=1, source_target_pairs={{0,8},{8,16},{16,24},{24,28},{28,20},{20,12},{12,4},{4,0},{1,9},{9... | collective-permute-start | bytes 393224 | tf_op jit(solution)/shard_map/ppermute | solution.py:166
  81.1 0.8 collective-permute-start.31
  81.9 0.8 collective-permute-done.16.refs_7_
  82.7 5.8 %copy-done.3 = bf16[2048,4096]{1,0:T(8,128)(2,1)S(1)} copy-done((bf16[2048,4096]{1,0:T(8,128)(2,1)S(1)}, bf16[2048,4096]{1,0:T(8,128)(2,1)}, u32[]{:S(2)}) %copy-start.3) | copy-done | bytes 16777240
  88.5 5.0 %shard_map.78 = f32[2048,128]{1,0:T(8,128)S(1)} custom-call(s32[16]{0:T(128)S(1)} %dynamic-slice_bitcast_fusion.ids, bf16[512,128]{1,0:T(8,128)(2,1)S(1)} %add_convert_fusion.1.refs_0_, bf16[512,128]{1,0:T(8,128)(2,1)S(1)} %collective-permute-done.10.refs_1_, bf16[512,128]{1,0:T(8,128)(2,1)S(1)} %collective-permute-done.11.refs_2_, ...), custom_call_target="tpu_custom_call" | custom-call | flops 2147483648 | bytes 16777216 | tf_op jit(solution)/shard_map/pallas_call | solution.py:120
  93.6 0.8 collective-permute-start.34
  94.4 1.4 %collective-permute-start.35 = (bf16[512,128]{1,0:T(8,128)(2,1)S(1)}, bf16[512,128]{1,0:T(8,128)(2,1)S(1)}, u32[]{:S(2)}, u32[]{:S(2)}) collective-permute-start(bf16[512,128]{1,0:T(8,128)(2,1)S(1)} %collective-permute-done.31.refs_0_), channel_id=1, source_target_pairs={{0,4},{8,0},{16,8},{24,16},{28,24},{20,28},{12,20},{4,12},{1,5},{9... | collective-permute-start | bytes 393224 | tf_op jit(solution)/shard_map/ppermute | solution.py:166
  95.8 3.4 %shard_map.85.refs_3_ = f32[2048,128]{1,0:T(8,128)S(1)} custom-call(s32[16]{0:T(128)S(1)} %dynamic-slice_bitcast_fusion.ids, bf16[512,128]{1,0:T(8,128)(2,1)S(1)} %add_convert_fusion.refs_0_, bf16[512,128]{1,0:T(8,128)(2,1)S(1)} %collective-permute-done.29.refs_1_, bf16[512,128]{1,0:T(8,128)(2,1)S(1)} %collective-permute-done.32.refs_2_, ...), custom_call_target="tpu_custom_call" | custom-call | flops 1342177280 | bytes 10485760 | tf_op jit(solution)/shard_map/pallas_call | solution.py:120
  99.2 0.6 collective-permute-done.34.refs_1_
  100.0 2.3 %shard_map.86 = f32[2048,128]{1,0:T(8,128)S(1)} custom-call(s32[16]{0:T(128)S(1)} %dynamic-slice_bitcast_fusion.ids, bf16[512,128]{1,0:T(8,128)(2,1)S(1)} %collective-permute-done.31.refs_0_, bf16[512,128]{1,0:T(8,128)(2,1)S(1)} %collective-permute-done.34.refs_1_, bf16[512,128]{1,0:T(8,128)(2,1)S(1)} %collective-permute-done.35.refs_2_, ...), custom_call_target="tpu_custom_call" | custom-call | flops 805306368 | bytes 6291456 | tf_op jit(solution)/shard_map/pallas_call | solution.py:120
  102.5 1.6 %collective-permute-start.18 = (f32[512,128]{1,0:T(8,128)S(1)}, f32[512,128]{1,0:T(8,128)S(1)}, u32[]{:S(2)}, u32[]{:S(2)}) collective-permute-start(f32[512,128]{1,0:T(8,128)S(1)} %slice.35), channel_id=1, source_target_pairs={{0,2},{1,3},{2,0},{3,1},{4,6},{5,7},{6,4},{7,5},{8,10},{9,11},{10,... | collective-permute-start | bytes 786440 | tf_op jit(solution)/shard_map/ppermute | solution.py:169
  104.4 0.7 fusion
  105.1 1.5 %collective-permute-start.37 = (f32[512,128]{1,0:T(8,128)S(1)}, f32[512,128]{1,0:T(8,128)S(1)}, u32[]{:S(2)}, u32[]{:S(2)}) collective-permute-start(f32[512,128]{1,0:T(8,128)S(1)} %get-tuple-element.37), channel_id=1, source_target_pairs={{0,2},{1,3},{2,0},{3,1},{4,6},{5,7},{6,4},{7,5},{8,10},{9,11},{10,... | collective-permute-start | bytes 786440 | tf_op jit(solution)/shard_map/ppermute | solution.py:169
  106.6 5.1 %collective-permute-done.18 = f32[512,128]{1,0:T(8,128)S(1)} collective-permute-done((f32[512,128]{1,0:T(8,128)S(1)}, f32[512,128]{1,0:T(8,128)S(1)}, u32[]{:S(2)}, u32[]{:S(2)}) %collective-permute-start.18) | collective-permute-done | bytes 262176 | tf_op jit(solution)/shard_map/ppermute | solution.py:169
  111.7 0.7 slice_add_fusion.2.out_ref
  112.4 4.5 %collective-permute-done.37.arrived_ref = f32[512,128]{1,0:T(8,128)S(1)} collective-permute-done((f32[512,128]{1,0:T(8,128)S(1)}, f32[512,128]{1,0:T(8,128)S(1)}, u32[]{:S(2)}, u32[]{:S(2)}) %collective-permute-start.37) | collective-permute-done | bytes 262176 | tf_op jit(solution)/shard_map/ppermute | solution.py:169
  116.9 0.7 copy-done.6
  117.6 1.9 %shard_map.87 = f32[8,512]{1,0:T(8,128)} custom-call(f32[512,128]{1,0:T(8,128)} %slice_add_fusion.2.out_ref, f32[512,128]{1,0:T(8,128)} %get-tuple-element.38.in_ref, f32[512,128]{1,0:T(8,128)} %copy-done.6), custom_call_target="tpu_custom_call" | custom-call | tf_op jit(solution)/shard_map/pallas_call | solution.py:141
  (81 shorter events, 4.8 us)
Async XLA Ops:
  0.0 6.1 %collective-permute-start = (bf16[512,128]{1,0:T(8,128)(2,1)}, bf16[512,128]{1,0:T(8,128)(2,1)S(1)}, u32[]{:S(2)}, u32[]{:S(2)}) collective-permute-start(bf16[512,128]{1,0:T(8,128)(2,1)} %refs_0_.1), channel_id=1, source_target_pairs={{0,1},{1,0},{2,3},{3,2},{4,5},{5,4},{6,7},{7,6},{8,9},{9,8},{10,11... | collective-permute-start | bytes 393224 | tf_op jit(solution)/shard_map/ppermute | solution.py:169
  0.5 7.0 %collective-permute-start.1 = (bf16[512,128]{1,0:T(8,128)(2,1)}, bf16[512,128]{1,0:T(8,128)(2,1)S(1)}, u32[]{:S(2)}, u32[]{:S(2)}) collective-permute-start(bf16[512,128]{1,0:T(8,128)(2,1)} %refs_0_.1), channel_id=1, source_target_pairs={{0,2},{1,3},{2,0},{3,1},{4,6},{5,7},{6,4},{7,5},{8,10},{9,11},{10,... | collective-permute-start | bytes 393224 | tf_op jit(solution)/shard_map/ppermute | solution.py:169
  2.9 7.0 %collective-permute-start.2 = (bf16[512,128]{1,0:T(8,128)(2,1)}, bf16[512,128]{1,0:T(8,128)(2,1)S(1)}, u32[]{:S(2)}, u32[]{:S(2)}) collective-permute-start(bf16[512,128]{1,0:T(8,128)(2,1)} %refs_0_.1), channel_id=1, source_target_pairs={{0,3},{1,2},{2,1},{3,0},{4,7},{5,6},{6,5},{7,4},{8,11},{9,10},{10,... | collective-permute-start | bytes 393224 | tf_op jit(solution)/shard_map/ppermute | solution.py:169
  3.1 0.9 copy-start.4
  4.0 16.9 %collective-permute-start.19 = (bf16[512,128]{1,0:T(8,128)(2,1)S(1)}, bf16[512,128]{1,0:T(8,128)(2,1)S(1)}, u32[]{:S(2)}, u32[]{:S(2)}) collective-permute-start(bf16[512,128]{1,0:T(8,128)(2,1)S(1)} %shard_map.79.refs_0_), channel_id=1, source_target_pairs={{0,1},{1,0},{2,3},{3,2},{4,5},{5,4},{6,7},{7,6},{8,9},{9,8},{10,11... | collective-permute-start | bytes 393224 | tf_op jit(solution)/shard_map/ppermute | solution.py:169
  4.2 16.8 %collective-permute-start.20 = (bf16[512,128]{1,0:T(8,128)(2,1)S(1)}, bf16[512,128]{1,0:T(8,128)(2,1)S(1)}, u32[]{:S(2)}, u32[]{:S(2)}) collective-permute-start(bf16[512,128]{1,0:T(8,128)(2,1)S(1)} %shard_map.79.refs_0_), channel_id=1, source_target_pairs={{0,2},{1,3},{2,0},{3,1},{4,6},{5,7},{6,4},{7,5},{8,10},{9,11},{10,... | collective-permute-start | bytes 393224 | tf_op jit(solution)/shard_map/ppermute | solution.py:169
  6.1 14.9 %collective-permute-start.21 = (bf16[512,128]{1,0:T(8,128)(2,1)S(1)}, bf16[512,128]{1,0:T(8,128)(2,1)S(1)}, u32[]{:S(2)}, u32[]{:S(2)}) collective-permute-start(bf16[512,128]{1,0:T(8,128)(2,1)S(1)} %shard_map.79.refs_0_), channel_id=1, source_target_pairs={{0,3},{1,2},{2,1},{3,0},{4,7},{5,6},{6,5},{7,4},{8,11},{9,10},{10,... | collective-permute-start | bytes 393224 | tf_op jit(solution)/shard_map/ppermute | solution.py:169
  9.9 0.9 copy-start.5
  11.6 5.8 %copy-start = (bf16[2048,4096]{1,0:T(8,128)(2,1)S(1)}, bf16[2048,4096]{1,0:T(8,128)(2,1)}, u32[]{:S(2)}) copy-start(bf16[2048,4096]{1,0:T(8,128)(2,1)} %inverse.11) | copy-start | bytes 50331652
  17.4 13.6 %slice-start = ((s8[16777216]{0:T(1024)(128)(4,1)}), s8[4194304]{0:T(1024)(128)(4,1)S(1)}, s32[]{:S(2)}) async-start(s8[16777216]{0:T(1024)(128)(4,1)} %bitcast.2), calls=%async_computation | async-start | bytes 8388608
  17.4 13.6 %slice-start.1 = ((s8[16777216]{0:T(1024)(128)(4,1)}), s8[4194304]{0:T(1024)(128)(4,1)S(1)}, s32[]{:S(2)}) async-start(s8[16777216]{0:T(1024)(128)(4,1)} %bitcast.2), calls=%async_computation.1 | async-start | bytes 8388608
  18.8 17.1 %collective-permute-start.3 = (bf16[512,128]{1,0:T(8,128)(2,1)S(1)}, bf16[512,128]{1,0:T(8,128)(2,1)S(1)}, u32[]{:S(2)}, u32[]{:S(2)}) collective-permute-start(bf16[512,128]{1,0:T(8,128)(2,1)S(1)} %convert_element_type.48.refs_0_), channel_id=1, source_target_pairs={{0,8},{8,16},{16,24},{24,28},{28,20},{20,12},{12,4},{4,0},{1,9},{9... | collective-permute-start | bytes 393224 | tf_op jit(solution)/shard_map/ppermute | solution.py:166
  20.5 10.5 %slice-start.2 = ((s8[16777216]{0:T(1024)(128)(4,1)}), s8[4194304]{0:T(1024)(128)(4,1)S(1)}, s32[]{:S(2)}) async-start(s8[16777216]{0:T(1024)(128)(4,1)} %bitcast.2), calls=%async_computation.2 | async-start | bytes 8388608
  20.5 17.1 %collective-permute-start.7 = (bf16[512,128]{1,0:T(8,128)(2,1)S(1)}, bf16[512,128]{1,0:T(8,128)(2,1)S(1)}, u32[]{:S(2)}, u32[]{:S(2)}) collective-permute-start(bf16[512,128]{1,0:T(8,128)(2,1)S(1)} %convert_element_type.56), channel_id=1, source_target_pairs={{0,4},{8,0},{16,8},{24,16},{28,24},{20,28},{12,20},{4,12},{1,5},{9... | collective-permute-start | bytes 393224 | tf_op jit(solution)/shard_map/ppermute | solution.py:166
  21.7 5.8 %copy-start.1 = (bf16[2048,4096]{1,0:T(8,128)(2,1)S(1)}, bf16[2048,4096]{1,0:T(8,128)(2,1)}, u32[]{:S(2)}) copy-start(bf16[2048,4096]{1,0:T(8,128)(2,1)} %inverse.15) | copy-start | bytes 50331652
  27.4 3.5 %slice-start.3 = ((s8[16777216]{0:T(1024)(128)(4,1)}), s8[4194304]{0:T(1024)(128)(4,1)S(1)}, s32[]{:S(2)}) async-start(s8[16777216]{0:T(1024)(128)(4,1)} %bitcast.2), calls=%async_computation.3 | async-start | bytes 8388608
  27.4 7.0 %copy-start.2 = (bf16[2048,4096]{1,0:T(8,128)(2,1)S(1)}, bf16[2048,4096]{1,0:T(8,128)(2,1)}, u32[]{:S(2)}) copy-start(bf16[2048,4096]{1,0:T(8,128)(2,1)} %inverse.15) | copy-start | bytes 50331652
  28.8 14.5 %collective-permute-start.22 = (f32[512,128]{1,0:T(8,128)S(1)}, f32[512,128]{1,0:T(8,128)S(1)}, u32[]{:S(2)}, u32[]{:S(2)}) collective-permute-start(f32[512,128]{1,0:T(8,128)S(1)} %get-tuple-element.29.refs_0_), channel_id=1, source_target_pairs={{0,4},{8,0},{16,8},{24,16},{28,24},{20,28},{12,20},{4,12},{1,5},{9... | collective-permute-start | bytes 786440 | tf_op jit(solution)/shard_map/ppermute | solution.py:166
  30.4 14.8 %collective-permute-start.26 = (f32[512,128]{1,0:T(8,128)S(1)}, f32[512,128]{1,0:T(8,128)S(1)}, u32[]{:S(2)}, u32[]{:S(2)}) collective-permute-start(f32[512,128]{1,0:T(8,128)S(1)} %get-tuple-element.33), channel_id=1, source_target_pairs={{0,8},{8,16},{16,24},{24,28},{28,20},{20,12},{12,4},{4,0},{1,9},{9... | collective-permute-start | bytes 786440 | tf_op jit(solution)/shard_map/ppermute | solution.py:166
  35.9 5.7 %collective-permute-start.4 = (bf16[512,128]{1,0:T(8,128)(2,1)S(1)}, bf16[512,128]{1,0:T(8,128)(2,1)S(1)}, u32[]{:S(2)}, u32[]{:S(2)}) collective-permute-start(bf16[512,128]{1,0:T(8,128)(2,1)S(1)} %add_convert_fusion.6.refs_0_), channel_id=1, source_target_pairs={{0,8},{8,16},{16,24},{24,28},{28,20},{20,12},{12,4},{4,0},{1,9},{9... | collective-permute-start | bytes 393224 | tf_op jit(solution)/shard_map/ppermute | solution.py:166
  39.0 5.4 %collective-permute-start.8 = (bf16[512,128]{1,0:T(8,128)(2,1)S(1)}, bf16[512,128]{1,0:T(8,128)(2,1)S(1)}, u32[]{:S(2)}, u32[]{:S(2)}) collective-permute-start(bf16[512,128]{1,0:T(8,128)(2,1)S(1)} %add_convert_fusion.3), channel_id=1, source_target_pairs={{0,4},{8,0},{16,8},{24,16},{28,24},{20,28},{12,20},{4,12},{1,5},{9... | collective-permute-start | bytes 393224 | tf_op jit(solution)/shard_map/ppermute | solution.py:166
  41.6 11.4 %collective-permute-start.5 = (bf16[512,128]{1,0:T(8,128)(2,1)S(1)}, bf16[512,128]{1,0:T(8,128)(2,1)S(1)}, u32[]{:S(2)}, u32[]{:S(2)}) collective-permute-start(bf16[512,128]{1,0:T(8,128)(2,1)S(1)} %add_convert_fusion.5.refs_0_), channel_id=1, source_target_pairs={{0,8},{8,16},{16,24},{24,28},{28,20},{20,12},{12,4},{4,0},{1,9},{9... | collective-permute-start | bytes 393224 | tf_op jit(solution)/shard_map/ppermute | solution.py:166
  43.4 9.3 %collective-permute-start.23 = (f32[512,128]{1,0:T(8,128)S(1)}, f32[512,128]{1,0:T(8,128)S(1)}, u32[]{:S(2)}, u32[]{:S(2)}) collective-permute-start(f32[512,128]{1,0:T(8,128)S(1)} %add.68.refs_0_), channel_id=1, source_target_pairs={{0,4},{8,0},{16,8},{24,16},{28,24},{20,28},{12,20},{4,12},{1,5},{9... | collective-permute-start | bytes 786440 | tf_op jit(solution)/shard_map/ppermute | solution.py:166
  44.5 15.1 %collective-permute-start.9 = (bf16[512,128]{1,0:T(8,128)(2,1)S(1)}, bf16[512,128]{1,0:T(8,128)(2,1)S(1)}, u32[]{:S(2)}, u32[]{:S(2)}) collective-permute-start(bf16[512,128]{1,0:T(8,128)(2,1)S(1)} %add_convert_fusion.2), channel_id=1, source_target_pairs={{0,4},{8,0},{16,8},{24,16},{28,24},{20,28},{12,20},{4,12},{1,5},{9... | collective-permute-start | bytes 393224 | tf_op jit(solution)/shard_map/ppermute | solution.py:166
  45.3 9.6 %collective-permute-start.27 = (f32[512,128]{1,0:T(8,128)S(1)}, f32[512,128]{1,0:T(8,128)S(1)}, u32[]{:S(2)}, u32[]{:S(2)}) collective-permute-start(f32[512,128]{1,0:T(8,128)S(1)} %add.71), channel_id=1, source_target_pairs={{0,8},{8,16},{16,24},{24,28},{28,20},{20,12},{12,4},{4,0},{1,9},{9... | collective-permute-start | bytes 786440 | tf_op jit(solution)/shard_map/ppermute | solution.py:166
  52.7 6.5 %collective-permute-start.24 = (f32[512,128]{1,0:T(8,128)S(1)}, f32[512,128]{1,0:T(8,128)S(1)}, u32[]{:S(2)}, u32[]{:S(2)}) collective-permute-start(f32[512,128]{1,0:T(8,128)S(1)} %add.69.refs_0_), channel_id=1, source_target_pairs={{0,4},{8,0},{16,8},{24,16},{28,24},{20,28},{12,20},{4,12},{1,5},{9... | collective-permute-start | bytes 786440 | tf_op jit(solution)/shard_map/ppermute | solution.py:166
  53.0 6.6 %collective-permute-start.6 = (bf16[512,128]{1,0:T(8,128)(2,1)S(1)}, bf16[512,128]{1,0:T(8,128)(2,1)S(1)}, u32[]{:S(2)}, u32[]{:S(2)}) collective-permute-start(bf16[512,128]{1,0:T(8,128)(2,1)S(1)} %add_convert_fusion.4), channel_id=1, source_target_pairs={{0,8},{8,16},{16,24},{24,28},{28,20},{20,12},{12,4},{4,0},{1,9},{9... | collective-permute-start | bytes 393224 | tf_op jit(solution)/shard_map/ppermute | solution.py:166
  54.9 40.9 %slice-start.4 = ((s8[16777216]{0:T(1024)(128)(4,1)}), s8[4194304]{0:T(1024)(128)(4,1)S(1)}, s32[]{:S(2)}) async-start(s8[16777216]{0:T(1024)(128)(4,1)} %bitcast.4), calls=%async_computation.4 | async-start | bytes 8388608
  54.9 40.9 %slice-start.5 = ((s8[16777216]{0:T(1024)(128)(4,1)}), s8[4194304]{0:T(1024)(128)(4,1)S(1)}, s32[]{:S(2)}) async-start(s8[16777216]{0:T(1024)(128)(4,1)} %bitcast.4), calls=%async_computation.5 | async-start | bytes 8388608
  54.9 11.5 %collective-permute-start.28 = (f32[512,128]{1,0:T(8,128)S(1)}, f32[512,128]{1,0:T(8,128)S(1)}, u32[]{:S(2)}, u32[]{:S(2)}) collective-permute-start(f32[512,128]{1,0:T(8,128)S(1)} %add.72), channel_id=1, source_target_pairs={{0,8},{8,16},{16,24},{24,28},{28,20},{20,12},{12,4},{4,0},{1,9},{9... | collective-permute-start | bytes 786440 | tf_op jit(solution)/shard_map/ppermute | solution.py:166
  59.3 7.2 %collective-permute-start.25 = (f32[512,128]{1,0:T(8,128)S(1)}, f32[512,128]{1,0:T(8,128)S(1)}, u32[]{:S(2)}, u32[]{:S(2)}) collective-permute-start(f32[512,128]{1,0:T(8,128)S(1)} %add.70), channel_id=1, source_target_pairs={{0,4},{8,0},{16,8},{24,16},{28,24},{20,28},{12,20},{4,12},{1,5},{9... | collective-permute-start | bytes 786440 | tf_op jit(solution)/shard_map/ppermute | solution.py:166
  59.7 5.0 %collective-permute-start.10 = (bf16[512,128]{1,0:T(8,128)(2,1)S(1)}, bf16[512,128]{1,0:T(8,128)(2,1)S(1)}, u32[]{:S(2)}, u32[]{:S(2)}) collective-permute-start(bf16[512,128]{1,0:T(8,128)(2,1)S(1)} %add_convert_fusion.1.refs_0_), channel_id=1, source_target_pairs={{0,8},{8,16},{16,24},{24,28},{28,20},{20,12},{12,4},{4,0},{1,9},{9... | collective-permute-start | bytes 393224 | tf_op jit(solution)/shard_map/ppermute | solution.py:166
  61.5 7.4 %collective-permute-start.11 = (bf16[512,128]{1,0:T(8,128)(2,1)S(1)}, bf16[512,128]{1,0:T(8,128)(2,1)S(1)}, u32[]{:S(2)}, u32[]{:S(2)}) collective-permute-start(bf16[512,128]{1,0:T(8,128)(2,1)S(1)} %add_convert_fusion.1.refs_0_), channel_id=1, source_target_pairs={{0,4},{8,0},{16,8},{24,16},{28,24},{20,28},{12,20},{4,12},{1,5},{9... | collective-permute-start | bytes 393224 | tf_op jit(solution)/shard_map/ppermute | solution.py:166
  64.7 6.3 %collective-permute-start.12 = (bf16[512,128]{1,0:T(8,128)(2,1)S(1)}, bf16[512,128]{1,0:T(8,128)(2,1)S(1)}, u32[]{:S(2)}, u32[]{:S(2)}) collective-permute-start(bf16[512,128]{1,0:T(8,128)(2,1)S(1)} %collective-permute-done.10.refs_1_), channel_id=1, source_target_pairs={{0,8},{8,16},{16,24},{24,28},{28,20},{20,12},{12,4},{4,0},{1,9},{9... | collective-permute-start | bytes 393224 | tf_op jit(solution)/shard_map/ppermute | solution.py:166
  66.4 29.4 %slice-start.6 = ((s8[16777216]{0:T(1024)(128)(4,1)}), s8[4194304]{0:T(1024)(128)(4,1)S(1)}, s32[]{:S(2)}) async-start(s8[16777216]{0:T(1024)(128)(4,1)} %bitcast.4), calls=%async_computation.6 | async-start | bytes 8388608
  66.5 29.3 %slice-start.7 = ((s8[16777216]{0:T(1024)(128)(4,1)}), s8[4194304]{0:T(1024)(128)(4,1)S(1)}, s32[]{:S(2)}) async-start(s8[16777216]{0:T(1024)(128)(4,1)} %bitcast.4), calls=%async_computation.7 | async-start | bytes 8388608
  66.5 7.3 %collective-permute-start.29 = (bf16[512,128]{1,0:T(8,128)(2,1)S(1)}, bf16[512,128]{1,0:T(8,128)(2,1)S(1)}, u32[]{:S(2)}, u32[]{:S(2)}) collective-permute-start(bf16[512,128]{1,0:T(8,128)(2,1)S(1)} %add_convert_fusion.refs_0_), channel_id=1, source_target_pairs={{0,4},{8,0},{16,8},{24,16},{28,24},{20,28},{12,20},{4,12},{1,5},{9... | collective-permute-start | bytes 393224 | tf_op jit(solution)/shard_map/ppermute | solution.py:166
  68.8 6.3 %collective-permute-start.13 = (bf16[512,128]{1,0:T(8,128)(2,1)S(1)}, bf16[512,128]{1,0:T(8,128)(2,1)S(1)}, u32[]{:S(2)}, u32[]{:S(2)}) collective-permute-start(bf16[512,128]{1,0:T(8,128)(2,1)S(1)} %collective-permute-done.11.refs_2_), channel_id=1, source_target_pairs={{0,4},{8,0},{16,8},{24,16},{28,24},{20,28},{12,20},{4,12},{1,5},{9... | collective-permute-start | bytes 393224 | tf_op jit(solution)/shard_map/ppermute | solution.py:166
  71.0 6.7 %collective-permute-start.14 = (bf16[512,128]{1,0:T(8,128)(2,1)S(1)}, bf16[512,128]{1,0:T(8,128)(2,1)S(1)}, u32[]{:S(2)}, u32[]{:S(2)}) collective-permute-start(bf16[512,128]{1,0:T(8,128)(2,1)S(1)} %collective-permute-done.12.refs_3_), channel_id=1, source_target_pairs={{0,8},{8,16},{16,24},{24,28},{28,20},{20,12},{12,4},{4,0},{1,9},{9... | collective-permute-start | bytes 393224 | tf_op jit(solution)/shard_map/ppermute | solution.py:166
  72.1 7.8 %collective-permute-start.32 = (bf16[512,128]{1,0:T(8,128)(2,1)S(1)}, bf16[512,128]{1,0:T(8,128)(2,1)S(1)}, u32[]{:S(2)}, u32[]{:S(2)}) collective-permute-start(bf16[512,128]{1,0:T(8,128)(2,1)S(1)} %add_convert_fusion.refs_0_), channel_id=1, source_target_pairs={{0,8},{8,16},{16,24},{24,28},{28,20},{20,12},{12,4},{4,0},{1,9},{9... | collective-permute-start | bytes 393224 | tf_op jit(solution)/shard_map/ppermute | solution.py:166
  73.8 7.3 %collective-permute-start.30 = (bf16[512,128]{1,0:T(8,128)(2,1)S(1)}, bf16[512,128]{1,0:T(8,128)(2,1)S(1)}, u32[]{:S(2)}, u32[]{:S(2)}) collective-permute-start(bf16[512,128]{1,0:T(8,128)(2,1)S(1)} %collective-permute-done.29.refs_1_), channel_id=1, source_target_pairs={{0,4},{8,0},{16,8},{24,16},{28,24},{20,28},{12,20},{4,12},{1,5},{9... | collective-permute-start | bytes 393224 | tf_op jit(solution)/shard_map/ppermute | solution.py:166
  75.2 6.7 %collective-permute-start.15 = (bf16[512,128]{1,0:T(8,128)(2,1)S(1)}, bf16[512,128]{1,0:T(8,128)(2,1)S(1)}, u32[]{:S(2)}, u32[]{:S(2)}) collective-permute-start(bf16[512,128]{1,0:T(8,128)(2,1)S(1)} %collective-permute-done.13.refs_4_), channel_id=1, source_target_pairs={{0,4},{8,0},{16,8},{24,16},{28,24},{20,28},{12,20},{4,12},{1,5},{9... | collective-permute-start | bytes 393224 | tf_op jit(solution)/shard_map/ppermute | solution.py:166
  77.7 5.0 %collective-permute-start.16 = (bf16[512,128]{1,0:T(8,128)(2,1)S(1)}, bf16[512,128]{1,0:T(8,128)(2,1)S(1)}, u32[]{:S(2)}, u32[]{:S(2)}) collective-permute-start(bf16[512,128]{1,0:T(8,128)(2,1)S(1)} %collective-permute-done.14.refs_5_), channel_id=1, source_target_pairs={{0,8},{8,16},{16,24},{24,28},{28,20},{20,12},{12,4},{4,0},{1,9},{9... | collective-permute-start | bytes 393224 | tf_op jit(solution)/shard_map/ppermute | solution.py:166
  79.9 13.8 %collective-permute-start.33 = (bf16[512,128]{1,0:T(8,128)(2,1)S(1)}, bf16[512,128]{1,0:T(8,128)(2,1)S(1)}, u32[]{:S(2)}, u32[]{:S(2)}) collective-permute-start(bf16[512,128]{1,0:T(8,128)(2,1)S(1)} %collective-permute-done.32.refs_2_), channel_id=1, source_target_pairs={{0,8},{8,16},{16,24},{24,28},{28,20},{20,12},{12,4},{4,0},{1,9},{9... | collective-permute-start | bytes 393224 | tf_op jit(solution)/shard_map/ppermute | solution.py:166
  81.1 13.3 %collective-permute-start.31 = (bf16[512,128]{1,0:T(8,128)(2,1)S(1)}, bf16[512,128]{1,0:T(8,128)(2,1)S(1)}, u32[]{:S(2)}, u32[]{:S(2)}) collective-permute-start(bf16[512,128]{1,0:T(8,128)(2,1)S(1)} %collective-permute-done.30.refs_3_), channel_id=1, source_target_pairs={{0,4},{8,0},{16,8},{24,16},{28,24},{20,28},{12,20},{4,12},{1,5},{9... | collective-permute-start | bytes 393224 | tf_op jit(solution)/shard_map/ppermute | solution.py:166
  82.7 5.8 %copy-start.3 = (bf16[2048,4096]{1,0:T(8,128)(2,1)S(1)}, bf16[2048,4096]{1,0:T(8,128)(2,1)}, u32[]{:S(2)}) copy-start(bf16[2048,4096]{1,0:T(8,128)(2,1)} %refs_8_.1) | copy-start | bytes 50331652
  93.6 8.9 %collective-permute-start.17 = (f32[1024,128]{1,0:T(8,128)S(1)}, f32[1024,128]{1,0:T(8,128)S(1)}, u32[]{:S(2)}, u32[]{:S(2)}) collective-permute-start(f32[1024,128]{1,0:T(8,128)S(1)} %slice.33), channel_id=1, source_target_pairs={{0,1},{1,0},{2,3},{3,2},{4,5},{5,4},{6,7},{7,6},{8,9},{9,8},{10,11... | collective-permute-start | bytes 1572872 | tf_op jit(solution)/shard_map/ppermute | solution.py:169
  93.6 6.2 %collective-permute-start.34 = (bf16[512,128]{1,0:T(8,128)(2,1)S(1)}, bf16[512,128]{1,0:T(8,128)(2,1)S(1)}, u32[]{:S(2)}, u32[]{:S(2)}) collective-permute-start(bf16[512,128]{1,0:T(8,128)(2,1)S(1)} %collective-permute-done.33.refs_4_), channel_id=1, source_target_pairs={{0,8},{8,16},{16,24},{24,28},{28,20},{20,12},{12,4},{4,0},{1,9},{9... | collective-permute-start | bytes 393224 | tf_op jit(solution)/shard_map/ppermute | solution.py:166
  94.4 5.6 %collective-permute-start.35 = (bf16[512,128]{1,0:T(8,128)(2,1)S(1)}, bf16[512,128]{1,0:T(8,128)(2,1)S(1)}, u32[]{:S(2)}, u32[]{:S(2)}) collective-permute-start(bf16[512,128]{1,0:T(8,128)(2,1)S(1)} %collective-permute-done.31.refs_0_), channel_id=1, source_target_pairs={{0,4},{8,0},{16,8},{24,16},{28,24},{20,28},{12,20},{4,12},{1,5},{9... | collective-permute-start | bytes 393224 | tf_op jit(solution)/shard_map/ppermute | solution.py:166
  102.4 2.0 %collective-permute-start.36 = (f32[1024,128]{1,0:T(8,128)S(1)}, f32[1024,128]{1,0:T(8,128)S(1)}, u32[]{:S(2)}, u32[]{:S(2)}) collective-permute-start(f32[1024,128]{1,0:T(8,128)S(1)} %slice.37), channel_id=1, source_target_pairs={{0,1},{1,0},{2,3},{3,2},{4,5},{5,4},{6,7},{7,6},{8,9},{9,8},{10,11... | collective-permute-start | bytes 1572872 | tf_op jit(solution)/shard_map/ppermute | solution.py:169
  102.5 9.2 %collective-permute-start.18 = (f32[512,128]{1,0:T(8,128)S(1)}, f32[512,128]{1,0:T(8,128)S(1)}, u32[]{:S(2)}, u32[]{:S(2)}) collective-permute-start(f32[512,128]{1,0:T(8,128)S(1)} %slice.35), channel_id=1, source_target_pairs={{0,2},{1,3},{2,0},{3,1},{4,6},{5,7},{6,4},{7,5},{8,10},{9,11},{10,... | collective-permute-start | bytes 786440 | tf_op jit(solution)/shard_map/ppermute | solution.py:169
  105.1 11.8 %collective-permute-start.37 = (f32[512,128]{1,0:T(8,128)S(1)}, f32[512,128]{1,0:T(8,128)S(1)}, u32[]{:S(2)}, u32[]{:S(2)}) collective-permute-start(f32[512,128]{1,0:T(8,128)S(1)} %get-tuple-element.37), channel_id=1, source_target_pairs={{0,2},{1,3},{2,0},{3,1},{4,6},{5,7},{6,4},{7,5},{8,10},{9,11},{10,... | collective-permute-start | bytes 786440 | tf_op jit(solution)/shard_map/ppermute | solution.py:169
  116.9 0.7 copy-start.6

commit v2 on v1

v2 whole, which is shorter than its diff:
```python
import functools

import jax
import jax.numpy as jnp
import numpy as np
from jax import lax
from jax.experimental import pallas as pl
from jax.experimental.pallas import tpu as pltpu
from jax.sharding import PartitionSpec as P

QUERIES = 8
RANK = 16
LANES = 128
F32 = jnp.float32
BF16 = jnp.bfloat16
GRANT = 4 << 20
COST = 2
VMEM = pl.BlockSpec(memory_space=pltpu.VMEM)
SMEM = pl.BlockSpec(memory_space=pltpu.SMEM)
HBM = pl.BlockSpec(memory_space=pltpu.HBM)
EARLY = 1 << 10
LATE = 6 << 20
MARKS_A = {}
MARKS_G = {1: 24 << 20, 2: 24 << 20}
ANY = pl.BlockSpec(memory_space=pl.ANY)


def ring_order(size):
    rows = 1
    while rows * rows < size:
        rows *= 2
    cols = size // rows
    if rows * cols != size or cols < 2:
        return list(range(size))
    cycle = [(r, 0) for r in range(rows)]
    for i, r in enumerate(reversed(range(rows))):
        walk = range(1, cols) if i % 2 == 0 else range(cols - 1, 0, -1)
        cycle += [(r, c) for c in walk]
    return [r * cols + c for r, c in cycle]


def hbm(x):
    return pltpu.with_memory_space_constraint(x, pltpu.HBM)


def reversed_bits(j, bits):
    return sum(((j >> b) & 1) << (bits - 1 - b) for b in range(bits))


def partials_body(n, row, step, begin, more, along, ids, *refs):
    queries, refs = refs[:n], refs[n:]
    if more:
        sums, refs = refs[0], refs[1:]
    if along:
        (small, inverse, outs, small_out), refs = refs[:4], refs[4:]
    else:
        (inverse, outs), refs = refs[:2], refs[2:]
    held, arrived = refs
    height, (count, width) = queries[0].shape[0], outs.shape[:2]
    copies = []
    for b in range(count):
        columns = pl.ds(pl.multiple_of(ids[step + begin + b] * width, width), width)
        for k in range(n):
            rows = pl.ds(pl.multiple_of(ids[row + k] * height, height), height)
            copy = pltpu.make_async_copy(inverse.at[rows, columns], held.at[b, pl.ds(k * height, height), :], arrived.at[b, k])
            copy.start()
            copies.append(copy)
    if along:
        small_out[...] = small[...]
    turned = jnp.concatenate([query[...].T for query in queries], axis=1)
    for b in range(count):
        for copy in copies[b * n : (b + 1) * n]:
            copy.wait()
        part = jnp.dot(turned, held[b], preferred_element_type=F32).T
        outs[b] = part + sums[begin + b] if more else part


def partials(ids, inverse, queries, row, step, begin, count, width, sums=None, along=None, cost=1024):
    n, height, more = len(queries), queries[0].shape[0], sums is not None
    extra = [] if along is None else [along]
    shapes = [jax.ShapeDtypeStruct((count, width, LANES), F32)] + [jax.ShapeDtypeStruct(x.shape, x.dtype) for x in extra]
    return pl.pallas_call(
        functools.partial(partials_body, n, row, step, begin, more, along is not None),
        in_specs=[SMEM] + [VMEM] * (n + more + len(extra)) + [HBM],
        out_specs=[VMEM] * len(shapes),
        out_shape=shapes,
        scratch_shapes=[
            pltpu.VMEM((count, n * height, width), BF16),
            pltpu.SemaphoreType.DMA((count, n)),
        ],
        compiler_params=pltpu.CompilerParams(vmem_limit_bytes=2 * n * height * count * width + (6 << 20)),
        cost_estimate=pl.CostEstimate(flops=0, bytes_accessed=cost, transcendentals=0),
    )(ids, *queries, *([sums] if more else []), *extra, hbm(inverse))


def mark_body(small, out):
    out[...] = small[...]


def mark(small, cost):
    return pl.pallas_call(
        mark_body,
        in_specs=[VMEM],
        out_specs=VMEM,
        out_shape=jax.ShapeDtypeStruct(small.shape, small.dtype),
        compiler_params=pltpu.CompilerParams(vmem_limit_bytes=GRANT),
        cost_estimate=pl.CostEstimate(flops=0, bytes_accessed=cost, transcendentals=0),
    )(small)


def project_body(columns, first, tile, count, ids, *refs):
    n, (out, tick) = len(columns), refs[-2:]
    tick[...] = jnp.zeros_like(tick)
    factors, total = refs[:n], None if first else refs[n]
    tokens = refs[n + (not first)]
    height = tokens.shape[0] // count
    for j in range(count):
        rows = slice(j * height, (j + 1) * height)
        here = pl.ds(pl.multiple_of(ids[tile + j] * height, height), height)
        acc = None if first else total[rows, :]
        for column, factor in zip(columns, factors):
            width = factor.shape[0]
            block = tokens[here, pl.ds(pl.multiple_of(ids[column] * width, width), width)]
            term = jnp.dot(block, factor[...], preferred_element_type=F32)
            acc = term if acc is None else acc + term
        out[rows, :] = acc


def project(ids, columns, factors, total, tokens, tile, count, waits=()):
    n, first = len(factors), total is None
    rows, width = tokens.shape[0], factors[0].shape[0]
    return pl.pallas_call(
        functools.partial(project_body, columns, first, tile, count),
        in_specs=[SMEM] + [VMEM] * (n + (not first) + 1) + [ANY] * len(waits),
        out_specs=[VMEM, VMEM],
        out_shape=[jax.ShapeDtypeStruct((rows, LANES), F32), jax.ShapeDtypeStruct((8, LANES), F32)],
        compiler_params=pltpu.CompilerParams(vmem_limit_bytes=GRANT),
        cost_estimate=pl.CostEstimate(
            flops=2 * n * rows * width * LANES,
            bytes_accessed=COST * n * rows * width,
            transcendentals=0,
        ),
    )(ids, *factors, *([] if first else [total]), tokens, *waits)


def score_body(out_ref, in_ref, arrived_ref, scores_ref):
    product = out_ref[...] * (in_ref[...] + arrived_ref[...].astype(F32))
    scores_ref[...] = product.T.reshape(QUERIES, RANK, product.shape[0]).sum(axis=1)


def score(out_proj, in_proj, arrived):
    rows = out_proj.shape[0]
    return pl.pallas_call(
        score_body,
        in_specs=[VMEM] * 3,
        out_specs=VMEM,
        out_shape=jax.ShapeDtypeStruct((QUERIES, rows), F32),
    )(
        out_proj, in_proj, arrived
    )


def program(tok, wid, g_inverse, a_inverse, query_out, query_in, output_grads, activations):
    bits = wid.bit_length() - 1
    cycle = ring_order(tok)
    width = g_inverse.shape[1] // tok
    height = g_inverse.shape[0] // wid
    share = output_grads.shape[0] // wid
    ahead, behind = tok // 2, (tok - 1) // 2
    sides = max(ahead, behind + 1)
    kernels = width % LANES == 0 and height % LANES == 0 and share % LANES == 0

    row_at, tile_at, step_at = tok, tok + wid, tok + 2 * wid
    table = np.zeros((tok, wid, 3 * tok + 2 * wid), np.int32)
    order = {way: [way * o % tok for k in range(tok // 2) for o in (tok // 2 - k, k - (tok - 1) // 2)] for way in (1, -1)}
    for t in range(tok):
        for w in range(wid):
            table[t, w, :tok] = (cycle.index(t) + np.arange(tok)) % tok
            table[t, w, row_at:tile_at] = w ^ np.arange(wid)
            table[t, w, tile_at:step_at] = [w ^ reversed_bits(j, bits) for j in range(wid)]
            table[t, w, step_at:] = table[t, w, order[1] + order[-1]]
    ids = jnp.asarray(table)[lax.axis_index("tok"), lax.axis_index("wid")]

    def shift(x, step):
        return lax.ppermute(x, "tok", [(cycle[i], cycle[(i + step) % tok]) for i in range(tok)])

    def swap(x, mask):
        return lax.ppermute(x, "wid", [(w, w ^ mask) for w in range(wid)])

    def at(offset):
        return offset % tok

    def gather_query(query):
        return [query] + [swap(query, k) for k in range(1, wid)]

    def make_partials(inverse, queries, columns):
        outs = []
        for column in columns:
            cut = lax.dynamic_slice_in_dim(inverse, ids[column] * width, width, 1)
            total = 0
            for k, query in enumerate(queries):
                block = lax.dynamic_slice_in_dim(cut, ids[row_at + k] * height, height, 0)
                total += lax.dot_general(block, query, (((0,), (0,)), ((), ())), preferred_element_type=F32)
            outs.append(total)
        return outs

    def make_project(tokens, columns, factors, total):
        outs = []
        for j in range(wid):
            cut = lax.dynamic_slice_in_dim(tokens, ids[tile_at + j] * share, share, 0)
            part = 0 if total is None else total[j * share : (j + 1) * share]
            for factor, column in zip(factors, columns):
                block = lax.dynamic_slice_in_dim(cut, ids[column] * width, width, 1)
                part += jnp.dot(block, factor, preferred_element_type=F32)
            outs.append(part)
        return jnp.concatenate(outs, axis=0)

    def end_partials(inverse, queries, sums, way, cost):
        half, step = 0 if sums is None else wid // 2, step_at + (tok if way < 0 else 0)
        (one,) = partials(ids, inverse, queries[half:], row_at + half, step, 0, 2, width, sums, cost=cost)
        (two,) = partials(ids, inverse, queries[half:], row_at + half, step, 2, tok - 2, width, sums, cost=cost)
        return [one[0], one[1]] + [two[i] for i in range(tok - 2)]

    def precondition(terms, way, narrow, marks):
        fwd, bwd = terms[0::2], terms[1::2]
        front, back = fwd[0], bwd[0]
        for k in range(1, sides + 1):
            if k <= ahead:
                front = shift(front.astype(BF16 if k <= narrow else F32), way).astype(F32)
            if k <= behind:
                back = shift(back.astype(BF16 if k < narrow or narrow >= ahead else F32), -way).astype(F32)
            if k < ahead:
                front = front + fwd[k]
                if k in marks and kernels:
                    front = mark(front, marks[k])
            if k < behind:
                back = back + bwd[k]
        return (front + back + bwd[behind]).astype(BF16)

    def gather_project(tokens, factor, way, tied=True, waits=()):
        front = back = factor
        total = tick = None
        factors, columns = [factor], [at(0)]
        for k in range(1, ahead + 1):
            if tick is not None and tied:
                front = (front.astype(F32) + tick[:1]).astype(BF16)
                tick = None
            front = shift(front, way)
            if k <= behind:
                back = shift(back, -way)
            if k == ahead - 1 and kernels:
                total, tick = project(ids, columns, factors, total, tokens, tile_at, wid)
                factors, columns = [], []
            factors.append(front)
            columns.append(at(-way * k))
            if k <= behind:
                factors.append(back)
                columns.append(at(way * k))
        if kernels:
            return project(ids, columns, factors, total, tokens, tile_at, wid, waits)[0]
        return make_project(tokens, columns, factors, total)

    def scatter(total, last):
        for b in range(bits):
            half = total.shape[0] // 2
            arrived = swap(total[half:], 1 << b)
            if b == bits - 1 and not last:
                return total[:half], arrived
            total = total[:half] + arrived
        return total

    half = wid // 2
    q_in = gather_query(query_in)
    if kernels:
        a_half, query_out = partials(ids, a_inverse, q_in[:half], row_at, step_at, 0, tok, width, along=query_out)
        q_out = gather_query(query_out)
        a_terms = end_partials(a_inverse, q_in, a_half, 1, EARLY)
        g_terms = end_partials(g_inverse, q_out, None, -1, LATE)
    else:
        q_out = gather_query(query_out)
        a_terms = make_partials(a_inverse, q_in, order[1])
        g_terms = make_partials(g_inverse, q_out, order[-1])
    a_pre = precondition(a_terms, 1, ahead, MARKS_A)
    g_pre = precondition(g_terms, -1, ahead // 2, MARKS_G)
    in_proj = scatter(gather_project(activations, a_pre, 1), True)
    out_proj, arrived = scatter(gather_project(output_grads, g_pre, -1), False)
    return score(in_proj, out_proj, arrived)


def solution(mesh):
    return jax.shard_map(
        functools.partial(program, mesh.shape["tok"], mesh.shape["wid"]),
        mesh=mesh,
        in_specs=(
            P("tok", "wid"),
            P("tok", "wid"),
            P(("tok", "wid"), None),
            P(("tok", "wid"), None),
            P("tok", "wid"),
            P("tok", "wid"),
        ),
        out_specs=P(None, ("tok", "wid")),
        check_vma=False,
    )
```

time: 120 us -> 110 us (0.917)
  local copies, waits for them, and re-layouts: 23.5 us -> 4.12 us
  Pallas kernels: 25.1 us -> 36.8 us
  waiting for transfers between devices: 33 us -> 29 us
  starting transfers between devices: 36.2 us -> 38.4 us
    unnamed x30 -> x22, local copies, waits for them, and re-layouts: 22 us -> 2.55 us
    pallas_call x12 -> x8, Pallas kernels: 14.3 us -> 24.3 us  [the longest x5 22.4 us: partials(): pl.pallas_call(functools.partial(partials_body, n, row, step, begin, more...]
    ppermute x10, waiting for transfers between devices: 13 us -> 9.69 us  [swap(): return lax.ppermute(x, 'wid', [(w, w ^ mask) for w in range(wid)])]
    ppermute x28, starting transfers between devices: 27.9 us -> 30.2 us  [shift(): lax.ppermute(x, 'tok', [(cycle[i], cycle[(i + step) % tok]) for i in rang...]
    pallas_call x3 -> x4, Pallas kernels: 10.7 us -> 12.5 us  [project(): pl.pallas_call(functools.partial(project_body, columns, first, tile, coun...]
  transfers between devices with their start and end apart: 38 -> 38, of which waited for: 18 -> 15; matrix products, arithmetic and copies ran while one was open for 2% -> 3% of each run, Pallas kernels for 19% -> 29%
where the time goes in v2:
time: 110 us
  starting transfers between devices  38.4 us (35%)
  Pallas kernels  36.8 us (33%)
  waiting for transfers between devices  29 us (26%)
  local copies, waits for them, and re-layouts  4.12 us (4%)
  other arithmetic  1.38 us (1%)
    ppermute x28, starting transfers between devices, shift(): lax.ppermute(x, 'tok', [(cycle[i], cycle[(i + step) % tok]) for i in rang...  30.2 us
    pallas_call x5, Pallas kernels, partials(): pl.pallas_call(functools.partial(partials_body, n, row, step, begin, more...  22.4 us
    ppermute x28, waiting for transfers between devices, shift(): lax.ppermute(x, 'tok', [(cycle[i], cycle[(i + step) % tok]) for i in rang...  19.3 us
    pallas_call x4, Pallas kernels, project(): pl.pallas_call(functools.partial(project_body, columns, first, tile, coun...  12.5 us
    ppermute x10, waiting for transfers between devices, swap(): return lax.ppermute(x, 'wid', [(w, w ^ mask) for w in range(wid)])  9.69 us
    ppermute x10, starting transfers between devices, swap(): return lax.ppermute(x, 'wid', [(w, w ^ mask) for w in range(wid)])  8.25 us
    unnamed x22, local copies, waits for them, and re-layouts  2.55 us
  transfers between devices with their start and end apart: 38, of which 15 were waited for; matrix products, arithmetic and copies ran while one was open for 3% of the time, Pallas kernels for 29%

profile of v2, /device:TPU:0, one launch (start us, length us, event | category | flops | bytes accessed | tf_op | source)
XLA Modules:
  0.0 110.0 jit_solution(6327933456596179343)
XLA Ops:
  0.0 0.5 collective-permute-start.2
  0.5 2.5 %collective-permute-start = (bf16[512,128]{1,0:T(8,128)(2,1)}, bf16[512,128]{1,0:T(8,128)(2,1)S(1)}, u32[]{:S(2)}, u32[]{:S(2)}) collective-permute-start(bf16[512,128]{1,0:T(8,128)(2,1)} %refs_0_.1), channel_id=1, source_target_pairs={{0,2},{1,3},{2,0},{3,1},{4,6},{5,7},{6,4},{7,5},{8,10},{9,11},{10,... | collective-permute-start | bytes 393224 | tf_op jit(solution)/shard_map/ppermute | solution.py:188
  3.1 0.7 dynamic-slice_bitcast_fusion.ids
  3.8 0.9 copy-done
  4.7 0.9 copy-done.1
  5.6 5.2 %shard_map.73 = (f32[8,512,128]{2,1,0:T(8,128)S(1)}, bf16[512,128]{1,0:T(8,128)(2,1)S(1)}) custom-call(s32[32]{0:T(128)S(1)} %dynamic-slice_bitcast_fusion.ids, bf16[512,128]{1,0:T(8,128)(2,1)S(1)} %copy-done.1, bf16[512,128]{1,0:T(8,128)(2,1)S(1)} %collective-permute-done.2.refs_1_, bf16[512,128]{1,0:T(8,128)(2,1)S(1)} %copy-done, bf16[2048,4096]{1,0:T(8,128)(2,1)} %refs_3_.5), custom_call_target="tpu_custom_call" | custom-call | bytes 1024 | tf_op jit(solution)/shard_map/pallas_call | solution.py:82
  10.8 2.6 %shard_map.74 = f32[2,512,128]{2,1,0:T(8,128)S(1)} custom-call(s32[32]{0:T(128)S(1)} %dynamic-slice_bitcast_fusion.ids, bf16[512,128]{1,0:T(8,128)(2,1)S(1)} %collective-permute-done.refs_0_, bf16[512,128]{1,0:T(8,128)(2,1)S(1)} %collective-permute-done.1.refs_1_, f32[8,512,128]{2,1,0:T(8,128)S(1)} %get-tuple-element.13.refs_2_, bf16[2048,4096]{1,0:T(8,128)(2,1)} %refs_3_.5), custom_call_target="tpu_custom_call" | custom-call | bytes 1024 | tf_op jit(solution)/shard_map/pallas_call | solution.py:82
  13.5 1.8 %collective-permute-start.3 = (bf16[512,128]{1,0:T(8,128)(2,1)S(1)}, bf16[512,128]{1,0:T(8,128)(2,1)S(1)}, u32[]{:S(2)}, u32[]{:S(2)}) collective-permute-start(bf16[512,128]{1,0:T(8,128)(2,1)S(1)} %get-tuple-element.33), channel_id=1, source_target_pairs={{0,8},{8,16},{16,24},{24,28},{28,20},{20,12},{12,4},{4,0},{1,9},{9... | collective-permute-start | bytes 393224 | tf_op jit(solution)/shard_map/ppermute | solution.py:185
  15.4 1.5 %collective-permute-start.20 = (bf16[512,128]{1,0:T(8,128)(2,1)S(1)}, bf16[512,128]{1,0:T(8,128)(2,1)S(1)}, u32[]{:S(2)}, u32[]{:S(2)}) collective-permute-start(bf16[512,128]{1,0:T(8,128)(2,1)S(1)} %get-tuple-element.17.refs_0_), channel_id=1, source_target_pairs={{0,2},{1,3},{2,0},{3,1},{4,6},{5,7},{6,4},{7,5},{8,10},{9,11},{10,... | collective-permute-start | bytes 393224 | tf_op jit(solution)/shard_map/ppermute | solution.py:188
  16.8 0.4 collective-permute-start.21
  17.2 0.3 collective-permute-start.7
  17.5 4.3 %shard_map.75 = f32[6,512,128]{2,1,0:T(8,128)S(1)} custom-call(s32[32]{0:T(128)S(1)} %dynamic-slice_bitcast_fusion.ids, bf16[512,128]{1,0:T(8,128)(2,1)S(1)} %collective-permute-done.refs_0_, bf16[512,128]{1,0:T(8,128)(2,1)S(1)} %collective-permute-done.1.refs_1_, f32[8,512,128]{2,1,0:T(8,128)S(1)} %get-tuple-element.13.refs_2_, bf16[2048,4096]{1,0:T(8,128)(2,1)} %refs_3_.5), custom_call_target="tpu_custom_call" | custom-call | bytes 1024 | tf_op jit(solution)/shard_map/pallas_call | solution.py:82
  21.9 1.8 %collective-permute-start.4 = (bf16[512,128]{1,0:T(8,128)(2,1)S(1)}, bf16[512,128]{1,0:T(8,128)(2,1)S(1)}, u32[]{:S(2)}, u32[]{:S(2)}) collective-permute-start(bf16[512,128]{1,0:T(8,128)(2,1)S(1)} %fusion.18), channel_id=1, source_target_pairs={{0,8},{8,16},{16,24},{24,28},{28,20},{20,12},{12,4},{4,0},{1,9},{9... | collective-permute-start | bytes 393224 | tf_op jit(solution)/shard_map/ppermute | solution.py:185
  23.7 3.7 %shard_map.78 = f32[2,512,128]{2,1,0:T(8,128)S(1)} custom-call(s32[32]{0:T(128)S(1)} %dynamic-slice_bitcast_fusion.ids, bf16[512,128]{1,0:T(8,128)(2,1)S(1)} %get-tuple-element.17.refs_0_, bf16[512,128]{1,0:T(8,128)(2,1)S(1)} %collective-permute-done.19.refs_1_, bf16[512,128]{1,0:T(8,128)(2,1)S(1)} %collective-permute-done.20.refs_2_, ...), custom_call_target="tpu_custom_call" | custom-call | bytes 6291456 | tf_op jit(solution)/shard_map/pallas_call | solution.py:82
  27.5 1.6 %collective-permute-start.26 = (bf16[512,128]{1,0:T(8,128)(2,1)S(1)}, bf16[512,128]{1,0:T(8,128)(2,1)S(1)}, u32[]{:S(2)}, u32[]{:S(2)}) collective-permute-start(bf16[512,128]{1,0:T(8,128)(2,1)S(1)} %get-tuple-element.31), channel_id=1, source_target_pairs={{0,8},{8,16},{16,24},{24,28},{28,20},{20,12},{12,4},{4,0},{1,9},{9... | collective-permute-start | bytes 393224 | tf_op jit(solution)/shard_map/ppermute | solution.py:185
  29.1 0.5 collective-permute-start.22
  29.6 6.5 %shard_map.79 = f32[6,512,128]{2,1,0:T(8,128)S(1)} custom-call(s32[32]{0:T(128)S(1)} %dynamic-slice_bitcast_fusion.ids, bf16[512,128]{1,0:T(8,128)(2,1)S(1)} %get-tuple-element.17.refs_0_, bf16[512,128]{1,0:T(8,128)(2,1)S(1)} %collective-permute-done.19.refs_1_, bf16[512,128]{1,0:T(8,128)(2,1)S(1)} %collective-permute-done.20.refs_2_, ...), custom_call_target="tpu_custom_call" | custom-call | bytes 6291456 | tf_op jit(solution)/shard_map/pallas_call | solution.py:82
  36.2 1.6 %collective-permute-start.5 = (bf16[512,128]{1,0:T(8,128)(2,1)S(1)}, bf16[512,128]{1,0:T(8,128)(2,1)S(1)}, u32[]{:S(2)}, u32[]{:S(2)}) collective-permute-start(bf16[512,128]{1,0:T(8,128)(2,1)S(1)} %get-tuple-element.27), channel_id=1, source_target_pairs={{0,8},{8,16},{16,24},{24,28},{28,20},{20,12},{12,4},{4,0},{1,9},{9... | collective-permute-start | bytes 393224 | tf_op jit(solution)/shard_map/ppermute | solution.py:185
  37.8 0.5 collective-permute-start.8
  38.4 0.2 collective-permute-start.23
  38.6 2.6 %collective-permute-done.5 = bf16[512,128]{1,0:T(8,128)(2,1)S(1)} collective-permute-done((bf16[512,128]{1,0:T(8,128)(2,1)S(1)}, bf16[512,128]{1,0:T(8,128)(2,1)S(1)}, u32[]{:S(2)}, u32[]{:S(2)}) %collective-permute-start.5) | collective-permute-done | bytes 131104 | tf_op jit(solution)/shard_map/ppermute | solution.py:185
  41.2 2.6 %collective-permute-done.8 = bf16[512,128]{1,0:T(8,128)(2,1)S(1)} collective-permute-done((bf16[512,128]{1,0:T(8,128)(2,1)S(1)}, bf16[512,128]{1,0:T(8,128)(2,1)S(1)}, u32[]{:S(2)}, u32[]{:S(2)}) %collective-permute-start.8) | collective-permute-done | bytes 131104 | tf_op jit(solution)/shard_map/ppermute | solution.py:185
  43.9 0.5 collective-permute-start.9
  44.4 1.6 %collective-permute-start.6 = (bf16[512,128]{1,0:T(8,128)(2,1)S(1)}, bf16[512,128]{1,0:T(8,128)(2,1)S(1)}, u32[]{:S(2)}, u32[]{:S(2)}) collective-permute-start(bf16[512,128]{1,0:T(8,128)(2,1)S(1)} %get-tuple-element.25), channel_id=1, source_target_pairs={{0,8},{8,16},{16,24},{24,28},{28,20},{20,12},{12,4},{4,0},{1,9},{9... | collective-permute-start | bytes 393224 | tf_op jit(solution)/shard_map/ppermute | solution.py:185
  46.0 0.6 collective-permute-done.23
  46.6 1.7 %collective-permute-start.27 = (f32[512,128]{1,0:T(8,128)S(1)}, f32[512,128]{1,0:T(8,128)S(1)}, u32[]{:S(2)}, u32[]{:S(2)}) collective-permute-start(f32[512,128]{1,0:T(8,128)S(1)} %get-tuple-element.23), channel_id=1, source_target_pairs={{0,8},{8,16},{16,24},{24,28},{28,20},{20,12},{12,4},{4,0},{1,9},{9... | collective-permute-start | bytes 786440 | tf_op jit(solution)/shard_map/ppermute | solution.py:185
  48.3 0.5 collective-permute-start.24
  48.8 1.3 %collective-permute-done.9 = bf16[512,128]{1,0:T(8,128)(2,1)S(1)} collective-permute-done((bf16[512,128]{1,0:T(8,128)(2,1)S(1)}, bf16[512,128]{1,0:T(8,128)(2,1)S(1)}, u32[]{:S(2)}, u32[]{:S(2)}) %collective-permute-start.9) | collective-permute-done | bytes 131104 | tf_op jit(solution)/shard_map/ppermute | solution.py:185
  50.1 0.8 collective-permute-done.6
  50.9 1.6 %collective-permute-start.10 = (bf16[512,128]{1,0:T(8,128)(2,1)S(1)}, bf16[512,128]{1,0:T(8,128)(2,1)S(1)}, u32[]{:S(2)}, u32[]{:S(2)}) collective-permute-start(bf16[512,128]{1,0:T(8,128)(2,1)S(1)} %fusion.8.refs_0_), channel_id=1, source_target_pairs={{0,8},{8,16},{16,24},{24,28},{28,20},{20,12},{12,4},{4,0},{1,9},{9... | collective-permute-start | bytes 393224 | tf_op jit(solution)/shard_map/ppermute | solution.py:185
  52.6 0.5 collective-permute-start.13
  53.0 3.5 %collective-permute-done.10.refs_1_ = bf16[512,128]{1,0:T(8,128)(2,1)S(1)} collective-permute-done((bf16[512,128]{1,0:T(8,128)(2,1)S(1)}, bf16[512,128]{1,0:T(8,128)(2,1)S(1)}, u32[]{:S(2)}, u32[]{:S(2)}) %collective-permute-start.10) | collective-permute-done | bytes 131104 | tf_op jit(solution)/shard_map/ppermute | solution.py:185
  56.5 1.6 %collective-permute-start.11 = (bf16[512,128]{1,0:T(8,128)(2,1)S(1)}, bf16[512,128]{1,0:T(8,128)(2,1)S(1)}, u32[]{:S(2)}, u32[]{:S(2)}) collective-permute-start(bf16[512,128]{1,0:T(8,128)(2,1)S(1)} %collective-permute-done.10.refs_1_), channel_id=1, source_target_pairs={{0,8},{8,16},{16,24},{24,28},{28,20},{20,12},{12,4},{4,0},{1,9},{9... | collective-permute-start | bytes 393224 | tf_op jit(solution)/shard_map/ppermute | solution.py:185
  58.1 0.5 collective-permute-start.14
  58.6 0.5 collective-permute-start.25
  59.1 1.6 %collective-permute-start.28 = (f32[512,128]{1,0:T(8,128)S(1)}, f32[512,128]{1,0:T(8,128)S(1)}, u32[]{:S(2)}, u32[]{:S(2)}) collective-permute-start(f32[512,128]{1,0:T(8,128)S(1)} %get-tuple-element.21), channel_id=1, source_target_pairs={{0,8},{8,16},{16,24},{24,28},{28,20},{20,12},{12,4},{4,0},{1,9},{9... | collective-permute-start | bytes 786440 | tf_op jit(solution)/shard_map/ppermute | solution.py:185
  60.7 2.3 %collective-permute-done.11.refs_3_ = bf16[512,128]{1,0:T(8,128)(2,1)S(1)} collective-permute-done((bf16[512,128]{1,0:T(8,128)(2,1)S(1)}, bf16[512,128]{1,0:T(8,128)(2,1)S(1)}, u32[]{:S(2)}, u32[]{:S(2)}) %collective-permute-start.11) | collective-permute-done | bytes 131104 | tf_op jit(solution)/shard_map/ppermute | solution.py:185
  63.0 1.6 %collective-permute-start.12 = (bf16[512,128]{1,0:T(8,128)(2,1)S(1)}, bf16[512,128]{1,0:T(8,128)(2,1)S(1)}, u32[]{:S(2)}, u32[]{:S(2)}) collective-permute-start(bf16[512,128]{1,0:T(8,128)(2,1)S(1)} %collective-permute-done.11.refs_3_), channel_id=1, source_target_pairs={{0,8},{8,16},{16,24},{24,28},{28,20},{20,12},{12,4},{4,0},{1,9},{9... | collective-permute-start | bytes 393224 | tf_op jit(solution)/shard_map/ppermute | solution.py:185
  64.6 0.5 collective-permute-start.15
  65.1 3.4 %shard_map.76 = (f32[2048,128]{1,0:T(8,128)S(1)}, f32[8,128]{1,0:T(8,128)S(1)}) custom-call(s32[32]{0:T(128)S(1)} %dynamic-slice_bitcast_fusion.ids, bf16[512,128]{1,0:T(8,128)(2,1)S(1)} %fusion.8.refs_0_, bf16[512,128]{1,0:T(8,128)(2,1)S(1)} %collective-permute-done.10.refs_1_, bf16[512,128]{1,0:T(8,128)(2,1)S(1)} %collective-permute-done.13.refs_2_, ...), custom_call_target="tpu_custom_call" | custom-call | flops 1342177280 | bytes 10485760 | tf_op jit(solution)/shard_map/pallas_call | solution.py:132
  68.5 0.4 collective-permute-done.25
  68.9 0.5 collective-permute-start.29
  69.3 1.6 %collective-permute-start.32 = (bf16[512,128]{1,0:T(8,128)(2,1)S(1)}, bf16[512,128]{1,0:T(8,128)(2,1)S(1)}, u32[]{:S(2)}, u32[]{:S(2)}) collective-permute-start(bf16[512,128]{1,0:T(8,128)(2,1)S(1)} %fusion.1.refs_0_), channel_id=1, source_target_pairs={{0,8},{8,16},{16,24},{24,28},{28,20},{20,12},{12,4},{4,0},{1,9},{9... | collective-permute-start | bytes 393224 | tf_op jit(solution)/shard_map/ppermute | solution.py:185
  71.0 1.8 %collective-permute-start.16 = (bf16[512,128]{1,0:T(8,128)(2,1)S(1)}, bf16[512,128]{1,0:T(8,128)(2,1)S(1)}, u32[]{:S(2)}, u32[]{:S(2)}) collective-permute-start(bf16[512,128]{1,0:T(8,128)(2,1)S(1)} %add_convert_fusion.1), channel_id=1, source_target_pairs={{0,8},{8,16},{16,24},{24,28},{28,20},{20,12},{12,4},{4,0},{1,9},{9... | collective-permute-start | bytes 393224 | tf_op jit(solution)/shard_map/ppermute | solution.py:185
  72.8 1.1 %collective-permute-done.29.refs_1_ = bf16[512,128]{1,0:T(8,128)(2,1)S(1)} collective-permute-done((bf16[512,128]{1,0:T(8,128)(2,1)S(1)}, bf16[512,128]{1,0:T(8,128)(2,1)S(1)}, u32[]{:S(2)}, u32[]{:S(2)}) %collective-permute-start.29) | collective-permute-done | bytes 131104 | tf_op jit(solution)/shard_map/ppermute | solution.py:185
  73.9 0.8 collective-permute-start.30
  74.7 1.2 %collective-permute-start.33 = (bf16[512,128]{1,0:T(8,128)(2,1)S(1)}, bf16[512,128]{1,0:T(8,128)(2,1)S(1)}, u32[]{:S(2)}, u32[]{:S(2)}) collective-permute-start(bf16[512,128]{1,0:T(8,128)(2,1)S(1)} %collective-permute-done.32.refs_2_), channel_id=1, source_target_pairs={{0,8},{8,16},{16,24},{24,28},{28,20},{20,12},{12,4},{4,0},{1,9},{9... | collective-permute-start | bytes 393224 | tf_op jit(solution)/shard_map/ppermute | solution.py:185
  76.0 2.9 %shard_map.77 = (f32[2048,128]{1,0:T(8,128)S(1)}, f32[8,128]{1,0:T(8,128)}) custom-call(s32[32]{0:T(128)S(1)} %dynamic-slice_bitcast_fusion.ids, bf16[512,128]{1,0:T(8,128)(2,1)S(1)} %collective-permute-done.12.refs_0_, bf16[512,128]{1,0:T(8,128)(2,1)S(1)} %collective-permute-done.15.refs_1_, bf16[512,128]{1,0:T(8,128)(2,1)S(1)} %collective-permute-done.16.refs_2_, ...), custom_call_target="tpu_custom_call" | custom-call | flops 805306368 | bytes 6291456 | tf_op jit(solution)/shard_map/pallas_call | solution.py:132
  79.0 1.5 %collective-permute-start.31 = (bf16[512,128]{1,0:T(8,128)(2,1)S(1)}, bf16[512,128]{1,0:T(8,128)(2,1)S(1)}, u32[]{:S(2)}, u32[]{:S(2)}) collective-permute-start(bf16[512,128]{1,0:T(8,128)(2,1)S(1)} %collective-permute-done.30.refs_3_), channel_id=1, source_target_pairs={{0,4},{8,0},{16,8},{24,16},{28,24},{20,28},{12,20},{4,12},{1,5},{9... | collective-permute-start | bytes 393224 | tf_op jit(solution)/shard_map/ppermute | solution.py:185
  80.5 0.6 collective-permute-start.34
  81.1 3.4 %shard_map.82 = (f32[2048,128]{1,0:T(8,128)S(1)}, f32[8,128]{1,0:T(8,128)S(1)}) custom-call(s32[32]{0:T(128)S(1)} %dynamic-slice_bitcast_fusion.ids, bf16[512,128]{1,0:T(8,128)(2,1)S(1)} %fusion.1.refs_0_, bf16[512,128]{1,0:T(8,128)(2,1)S(1)} %collective-permute-done.29.refs_1_, bf16[512,128]{1,0:T(8,128)(2,1)S(1)} %collective-permute-done.32.refs_2_, ...), custom_call_target="tpu_custom_call" | custom-call | flops 1342177280 | bytes 10485760 | tf_op jit(solution)/shard_map/pallas_call | solution.py:132
  84.5 0.4 collective-permute-done.31.refs_0_
  84.9 1.5 %collective-permute-start.35 = (bf16[512,128]{1,0:T(8,128)(2,1)S(1)}, bf16[512,128]{1,0:T(8,128)(2,1)S(1)}, u32[]{:S(2)}, u32[]{:S(2)}) collective-permute-start(bf16[512,128]{1,0:T(8,128)(2,1)S(1)} %add_convert_fusion), channel_id=1, source_target_pairs={{0,4},{8,0},{16,8},{24,16},{28,24},{20,28},{12,20},{4,12},{1,5},{9... | collective-permute-start | bytes 393224 | tf_op jit(solution)/shard_map/ppermute | solution.py:185
  86.4 3.6 %collective-permute-done.35.refs_2_ = bf16[512,128]{1,0:T(8,128)(2,1)S(1)} collective-permute-done((bf16[512,128]{1,0:T(8,128)(2,1)S(1)}, bf16[512,128]{1,0:T(8,128)(2,1)S(1)}, u32[]{:S(2)}, u32[]{:S(2)}) %collective-permute-start.35) | collective-permute-done | bytes 131104 | tf_op jit(solution)/shard_map/ppermute | solution.py:185
  90.0 2.9 %shard_map.83 = (f32[2048,128]{1,0:T(8,128)S(1)}, f32[8,128]{1,0:T(8,128)}) custom-call(s32[32]{0:T(128)S(1)} %dynamic-slice_bitcast_fusion.ids, bf16[512,128]{1,0:T(8,128)(2,1)S(1)} %collective-permute-done.31.refs_0_, bf16[512,128]{1,0:T(8,128)(2,1)S(1)} %collective-permute-done.34.refs_1_, bf16[512,128]{1,0:T(8,128)(2,1)S(1)} %collective-permute-done.35.refs_2_, ...), custom_call_target="tpu_custom_call" | custom-call | flops 805306368 | bytes 6291456 | tf_op jit(solution)/shard_map/pallas_call | solution.py:132
  93.1 1.6 %collective-permute-start.18 = (f32[512,128]{1,0:T(8,128)S(1)}, f32[512,128]{1,0:T(8,128)S(1)}, u32[]{:S(2)}, u32[]{:S(2)}) collective-permute-start(f32[512,128]{1,0:T(8,128)S(1)} %slice.117), channel_id=1, source_target_pairs={{0,2},{1,3},{2,0},{3,1},{4,6},{5,7},{6,4},{7,5},{8,10},{9,11},{10,... | collective-permute-start | bytes 786440 | tf_op jit(solution)/shard_map/ppermute | solution.py:188
  94.7 0.2 collective-permute-done.36
  94.9 0.8 fusion.19
  95.7 1.5 %collective-permute-start.37 = (f32[512,128]{1,0:T(8,128)S(1)}, f32[512,128]{1,0:T(8,128)S(1)}, u32[]{:S(2)}, u32[]{:S(2)}) collective-permute-start(f32[512,128]{1,0:T(8,128)S(1)} %get-tuple-element.29), channel_id=1, source_target_pairs={{0,2},{1,3},{2,0},{3,1},{4,6},{5,7},{6,4},{7,5},{8,10},{9,11},{10,... | collective-permute-start | bytes 786440 | tf_op jit(solution)/shard_map/ppermute | solution.py:188
  97.3 5.0 %collective-permute-done.18 = f32[512,128]{1,0:T(8,128)S(1)} collective-permute-done((f32[512,128]{1,0:T(8,128)S(1)}, f32[512,128]{1,0:T(8,128)S(1)}, u32[]{:S(2)}, u32[]{:S(2)}) %collective-permute-start.18) | collective-permute-done | bytes 262176 | tf_op jit(solution)/shard_map/ppermute | solution.py:188
  102.3 0.7 slice_add_fusion.2.out_ref
  103.0 4.5 %collective-permute-done.37.arrived_ref = f32[512,128]{1,0:T(8,128)S(1)} collective-permute-done((f32[512,128]{1,0:T(8,128)S(1)}, f32[512,128]{1,0:T(8,128)S(1)}, u32[]{:S(2)}, u32[]{:S(2)}) %collective-permute-start.37) | collective-permute-done | bytes 262176 | tf_op jit(solution)/shard_map/ppermute | solution.py:188
  107.5 0.7 copy-done.2
  108.2 1.9 %shard_map.84 = f32[8,512]{1,0:T(8,128)} custom-call(f32[512,128]{1,0:T(8,128)} %slice_add_fusion.2.out_ref, f32[512,128]{1,0:T(8,128)} %get-tuple-element.30.in_ref, f32[512,128]{1,0:T(8,128)} %copy-done.2), custom_call_target="tpu_custom_call" | custom-call | tf_op jit(solution)/shard_map/pallas_call | solution.py:153
  (73 shorter events, 1.3 us)
Async XLA Ops:
  0.0 3.8 %collective-permute-start.2 = (bf16[512,128]{1,0:T(8,128)(2,1)}, bf16[512,128]{1,0:T(8,128)(2,1)S(1)}, u32[]{:S(2)}, u32[]{:S(2)}) collective-permute-start(bf16[512,128]{1,0:T(8,128)(2,1)} %refs_0_.1), channel_id=1, source_target_pairs={{0,1},{1,0},{2,3},{3,2},{4,5},{5,4},{6,7},{7,6},{8,9},{9,8},{10,11... | collective-permute-start | bytes 393224 | tf_op jit(solution)/shard_map/ppermute | solution.py:188
  0.5 10.3 %collective-permute-start = (bf16[512,128]{1,0:T(8,128)(2,1)}, bf16[512,128]{1,0:T(8,128)(2,1)S(1)}, u32[]{:S(2)}, u32[]{:S(2)}) collective-permute-start(bf16[512,128]{1,0:T(8,128)(2,1)} %refs_0_.1), channel_id=1, source_target_pairs={{0,2},{1,3},{2,0},{3,1},{4,6},{5,7},{6,4},{7,5},{8,10},{9,11},{10,... | collective-permute-start | bytes 393224 | tf_op jit(solution)/shard_map/ppermute | solution.py:188
  2.9 7.9 %collective-permute-start.1 = (bf16[512,128]{1,0:T(8,128)(2,1)}, bf16[512,128]{1,0:T(8,128)(2,1)S(1)}, u32[]{:S(2)}, u32[]{:S(2)}) collective-permute-start(bf16[512,128]{1,0:T(8,128)(2,1)} %refs_0_.1), channel_id=1, source_target_pairs={{0,3},{1,2},{2,1},{3,0},{4,7},{5,6},{6,5},{7,4},{8,11},{9,10},{10,... | collective-permute-start | bytes 393224 | tf_op jit(solution)/shard_map/ppermute | solution.py:188
  3.8 0.9 copy-start
  4.7 0.9 copy-start.1
  13.5 8.3 %collective-permute-start.3 = (bf16[512,128]{1,0:T(8,128)(2,1)S(1)}, bf16[512,128]{1,0:T(8,128)(2,1)S(1)}, u32[]{:S(2)}, u32[]{:S(2)}) collective-permute-start(bf16[512,128]{1,0:T(8,128)(2,1)S(1)} %get-tuple-element.33), channel_id=1, source_target_pairs={{0,8},{8,16},{16,24},{24,28},{28,20},{20,12},{12,4},{4,0},{1,9},{9... | collective-permute-start | bytes 393224 | tf_op jit(solution)/shard_map/ppermute | solution.py:185
  15.3 8.3 %collective-permute-start.19 = (bf16[512,128]{1,0:T(8,128)(2,1)S(1)}, bf16[512,128]{1,0:T(8,128)(2,1)S(1)}, u32[]{:S(2)}, u32[]{:S(2)}) collective-permute-start(bf16[512,128]{1,0:T(8,128)(2,1)S(1)} %get-tuple-element.17.refs_0_), channel_id=1, source_target_pairs={{0,1},{1,0},{2,3},{3,2},{4,5},{5,4},{6,7},{7,6},{8,9},{9,8},{10,11... | collective-permute-start | bytes 393224 | tf_op jit(solution)/shard_map/ppermute | solution.py:188
  15.4 8.3 %collective-permute-start.20 = (bf16[512,128]{1,0:T(8,128)(2,1)S(1)}, bf16[512,128]{1,0:T(8,128)(2,1)S(1)}, u32[]{:S(2)}, u32[]{:S(2)}) collective-permute-start(bf16[512,128]{1,0:T(8,128)(2,1)S(1)} %get-tuple-element.17.refs_0_), channel_id=1, source_target_pairs={{0,2},{1,3},{2,0},{3,1},{4,6},{5,7},{6,4},{7,5},{8,10},{9,11},{10,... | collective-permute-start | bytes 393224 | tf_op jit(solution)/shard_map/ppermute | solution.py:188
  16.8 6.8 %collective-permute-start.21 = (bf16[512,128]{1,0:T(8,128)(2,1)S(1)}, bf16[512,128]{1,0:T(8,128)(2,1)S(1)}, u32[]{:S(2)}, u32[]{:S(2)}) collective-permute-start(bf16[512,128]{1,0:T(8,128)(2,1)S(1)} %get-tuple-element.17.refs_0_), channel_id=1, source_target_pairs={{0,3},{1,2},{2,1},{3,0},{4,7},{5,6},{6,5},{7,4},{8,11},{9,10},{10,... | collective-permute-start | bytes 393224 | tf_op jit(solution)/shard_map/ppermute | solution.py:188
  17.2 18.9 %collective-permute-start.7 = (bf16[512,128]{1,0:T(8,128)(2,1)S(1)}, bf16[512,128]{1,0:T(8,128)(2,1)S(1)}, u32[]{:S(2)}, u32[]{:S(2)}) collective-permute-start(bf16[512,128]{1,0:T(8,128)(2,1)S(1)} %get-tuple-element.34), channel_id=1, source_target_pairs={{0,4},{8,0},{16,8},{24,16},{28,24},{20,28},{12,20},{4,12},{1,5},{9... | collective-permute-start | bytes 393224 | tf_op jit(solution)/shard_map/ppermute | solution.py:185
  21.9 14.3 %collective-permute-start.4 = (bf16[512,128]{1,0:T(8,128)(2,1)S(1)}, bf16[512,128]{1,0:T(8,128)(2,1)S(1)}, u32[]{:S(2)}, u32[]{:S(2)}) collective-permute-start(bf16[512,128]{1,0:T(8,128)(2,1)S(1)} %fusion.18), channel_id=1, source_target_pairs={{0,8},{8,16},{16,24},{24,28},{28,20},{20,12},{12,4},{4,0},{1,9},{9... | collective-permute-start | bytes 393224 | tf_op jit(solution)/shard_map/ppermute | solution.py:185
  23.7 41.3 %slice-start = ((s8[16777216]{0:T(1024)(128)(4,1)}), s8[4194304]{0:T(1024)(128)(4,1)S(1)}, s32[]{:S(2)}) async-start(s8[16777216]{0:T(1024)(128)(4,1)} %bitcast.76), calls=%async_computation | async-start | bytes 8388608
  23.7 41.3 %slice-start.1 = ((s8[16777216]{0:T(1024)(128)(4,1)}), s8[4194304]{0:T(1024)(128)(4,1)S(1)}, s32[]{:S(2)}) async-start(s8[16777216]{0:T(1024)(128)(4,1)} %bitcast.76), calls=%async_computation.1 | async-start | bytes 8388608
  27.5 18.5 %collective-permute-start.26 = (bf16[512,128]{1,0:T(8,128)(2,1)S(1)}, bf16[512,128]{1,0:T(8,128)(2,1)S(1)}, u32[]{:S(2)}, u32[]{:S(2)}) collective-permute-start(bf16[512,128]{1,0:T(8,128)(2,1)S(1)} %get-tuple-element.31), channel_id=1, source_target_pairs={{0,8},{8,16},{16,24},{24,28},{28,20},{20,12},{12,4},{4,0},{1,9},{9... | collective-permute-start | bytes 393224 | tf_op jit(solution)/shard_map/ppermute | solution.py:185
  29.1 35.9 %slice-start.2 = ((s8[16777216]{0:T(1024)(128)(4,1)}), s8[4194304]{0:T(1024)(128)(4,1)S(1)}, s32[]{:S(2)}) async-start(s8[16777216]{0:T(1024)(128)(4,1)} %bitcast.76), calls=%async_computation.2 | async-start | bytes 8388608
  29.1 35.9 %slice-start.3 = ((s8[16777216]{0:T(1024)(128)(4,1)}), s8[4194304]{0:T(1024)(128)(4,1)S(1)}, s32[]{:S(2)}) async-start(s8[16777216]{0:T(1024)(128)(4,1)} %bitcast.76), calls=%async_computation.3 | async-start | bytes 8388608
  29.1 9.2 %collective-permute-start.22 = (bf16[512,128]{1,0:T(8,128)(2,1)S(1)}, bf16[512,128]{1,0:T(8,128)(2,1)S(1)}, u32[]{:S(2)}, u32[]{:S(2)}) collective-permute-start(bf16[512,128]{1,0:T(8,128)(2,1)S(1)} %get-tuple-element.32), channel_id=1, source_target_pairs={{0,4},{8,0},{16,8},{24,16},{28,24},{20,28},{12,20},{4,12},{1,5},{9... | collective-permute-start | bytes 393224 | tf_op jit(solution)/shard_map/ppermute | solution.py:185
  36.2 5.0 %collective-permute-start.5 = (bf16[512,128]{1,0:T(8,128)(2,1)S(1)}, bf16[512,128]{1,0:T(8,128)(2,1)S(1)}, u32[]{:S(2)}, u32[]{:S(2)}) collective-permute-start(bf16[512,128]{1,0:T(8,128)(2,1)S(1)} %get-tuple-element.27), channel_id=1, source_target_pairs={{0,8},{8,16},{16,24},{24,28},{28,20},{20,12},{12,4},{4,0},{1,9},{9... | collective-permute-start | bytes 393224 | tf_op jit(solution)/shard_map/ppermute | solution.py:185
  37.8 6.0 %collective-permute-start.8 = (bf16[512,128]{1,0:T(8,128)(2,1)S(1)}, bf16[512,128]{1,0:T(8,128)(2,1)S(1)}, u32[]{:S(2)}, u32[]{:S(2)}) collective-permute-start(bf16[512,128]{1,0:T(8,128)(2,1)S(1)} %get-tuple-element.28), channel_id=1, source_target_pairs={{0,4},{8,0},{16,8},{24,16},{28,24},{20,28},{12,20},{4,12},{1,5},{9... | collective-permute-start | bytes 393224 | tf_op jit(solution)/shard_map/ppermute | solution.py:185
  38.4 8.2 %collective-permute-start.23 = (bf16[512,128]{1,0:T(8,128)(2,1)S(1)}, bf16[512,128]{1,0:T(8,128)(2,1)S(1)}, u32[]{:S(2)}, u32[]{:S(2)}) collective-permute-start(bf16[512,128]{1,0:T(8,128)(2,1)S(1)} %convert_element_type.101), channel_id=1, source_target_pairs={{0,4},{8,0},{16,8},{24,16},{28,24},{20,28},{12,20},{4,12},{1,5},{9... | collective-permute-start | bytes 393224 | tf_op jit(solution)/shard_map/ppermute | solution.py:185
  43.9 6.2 %collective-permute-start.9 = (bf16[512,128]{1,0:T(8,128)(2,1)S(1)}, bf16[512,128]{1,0:T(8,128)(2,1)S(1)}, u32[]{:S(2)}, u32[]{:S(2)}) collective-permute-start(bf16[512,128]{1,0:T(8,128)(2,1)S(1)} %get-tuple-element.26), channel_id=1, source_target_pairs={{0,4},{8,0},{16,8},{24,16},{28,24},{20,28},{12,20},{4,12},{1,5},{9... | collective-permute-start | bytes 393224 | tf_op jit(solution)/shard_map/ppermute | solution.py:185
  44.4 6.4 %collective-permute-start.6 = (bf16[512,128]{1,0:T(8,128)(2,1)S(1)}, bf16[512,128]{1,0:T(8,128)(2,1)S(1)}, u32[]{:S(2)}, u32[]{:S(2)}) collective-permute-start(bf16[512,128]{1,0:T(8,128)(2,1)S(1)} %get-tuple-element.25), channel_id=1, source_target_pairs={{0,8},{8,16},{16,24},{24,28},{28,20},{20,12},{12,4},{4,0},{1,9},{9... | collective-permute-start | bytes 393224 | tf_op jit(solution)/shard_map/ppermute | solution.py:185
  46.6 11.9 %collective-permute-start.27 = (f32[512,128]{1,0:T(8,128)S(1)}, f32[512,128]{1,0:T(8,128)S(1)}, u32[]{:S(2)}, u32[]{:S(2)}) collective-permute-start(f32[512,128]{1,0:T(8,128)S(1)} %get-tuple-element.23), channel_id=1, source_target_pairs={{0,8},{8,16},{16,24},{24,28},{28,20},{20,12},{12,4},{4,0},{1,9},{9... | collective-permute-start | bytes 786440 | tf_op jit(solution)/shard_map/ppermute | solution.py:185
  48.3 10.2 %collective-permute-start.24 = (f32[512,128]{1,0:T(8,128)S(1)}, f32[512,128]{1,0:T(8,128)S(1)}, u32[]{:S(2)}, u32[]{:S(2)}) collective-permute-start(f32[512,128]{1,0:T(8,128)S(1)} %shard_map.81), channel_id=1, source_target_pairs={{0,4},{8,0},{16,8},{24,16},{28,24},{20,28},{12,20},{4,12},{1,5},{9... | collective-permute-start | bytes 786440 | tf_op jit(solution)/shard_map/ppermute | solution.py:185
  50.9 5.6 %collective-permute-start.10 = (bf16[512,128]{1,0:T(8,128)(2,1)S(1)}, bf16[512,128]{1,0:T(8,128)(2,1)S(1)}, u32[]{:S(2)}, u32[]{:S(2)}) collective-permute-start(bf16[512,128]{1,0:T(8,128)(2,1)S(1)} %fusion.8.refs_0_), channel_id=1, source_target_pairs={{0,8},{8,16},{16,24},{24,28},{28,20},{20,12},{12,4},{4,0},{1,9},{9... | collective-permute-start | bytes 393224 | tf_op jit(solution)/shard_map/ppermute | solution.py:185
  52.6 5.5 %collective-permute-start.13 = (bf16[512,128]{1,0:T(8,128)(2,1)S(1)}, bf16[512,128]{1,0:T(8,128)(2,1)S(1)}, u32[]{:S(2)}, u32[]{:S(2)}) collective-permute-start(bf16[512,128]{1,0:T(8,128)(2,1)S(1)} %fusion.8.refs_0_), channel_id=1, source_target_pairs={{0,4},{8,0},{16,8},{24,16},{28,24},{20,28},{12,20},{4,12},{1,5},{9... | collective-permute-start | bytes 393224 | tf_op jit(solution)/shard_map/ppermute | solution.py:185
  56.5 6.4 %collective-permute-start.11 = (bf16[512,128]{1,0:T(8,128)(2,1)S(1)}, bf16[512,128]{1,0:T(8,128)(2,1)S(1)}, u32[]{:S(2)}, u32[]{:S(2)}) collective-permute-start(bf16[512,128]{1,0:T(8,128)(2,1)S(1)} %collective-permute-done.10.refs_1_), channel_id=1, source_target_pairs={{0,8},{8,16},{16,24},{24,28},{28,20},{20,12},{12,4},{4,0},{1,9},{9... | collective-permute-start | bytes 393224 | tf_op jit(solution)/shard_map/ppermute | solution.py:185
  58.1 6.4 %collective-permute-start.14 = (bf16[512,128]{1,0:T(8,128)(2,1)S(1)}, bf16[512,128]{1,0:T(8,128)(2,1)S(1)}, u32[]{:S(2)}, u32[]{:S(2)}) collective-permute-start(bf16[512,128]{1,0:T(8,128)(2,1)S(1)} %collective-permute-done.13.refs_2_), channel_id=1, source_target_pairs={{0,4},{8,0},{16,8},{24,16},{28,24},{20,28},{12,20},{4,12},{1,5},{9... | collective-permute-start | bytes 393224 | tf_op jit(solution)/shard_map/ppermute | solution.py:185
  58.6 10.2 %collective-permute-start.25 = (f32[512,128]{1,0:T(8,128)S(1)}, f32[512,128]{1,0:T(8,128)S(1)}, u32[]{:S(2)}, u32[]{:S(2)}) collective-permute-start(f32[512,128]{1,0:T(8,128)S(1)} %get-tuple-element.22), channel_id=1, source_target_pairs={{0,4},{8,0},{16,8},{24,16},{28,24},{20,28},{12,20},{4,12},{1,5},{9... | collective-permute-start | bytes 786440 | tf_op jit(solution)/shard_map/ppermute | solution.py:185
  59.1 9.7 %collective-permute-start.28 = (f32[512,128]{1,0:T(8,128)S(1)}, f32[512,128]{1,0:T(8,128)S(1)}, u32[]{:S(2)}, u32[]{:S(2)}) collective-permute-start(f32[512,128]{1,0:T(8,128)S(1)} %get-tuple-element.21), channel_id=1, source_target_pairs={{0,8},{8,16},{16,24},{24,28},{28,20},{20,12},{12,4},{4,0},{1,9},{9... | collective-permute-start | bytes 786440 | tf_op jit(solution)/shard_map/ppermute | solution.py:185
  63.0 8.0 %collective-permute-start.12 = (bf16[512,128]{1,0:T(8,128)(2,1)S(1)}, bf16[512,128]{1,0:T(8,128)(2,1)S(1)}, u32[]{:S(2)}, u32[]{:S(2)}) collective-permute-start(bf16[512,128]{1,0:T(8,128)(2,1)S(1)} %collective-permute-done.11.refs_3_), channel_id=1, source_target_pairs={{0,8},{8,16},{16,24},{24,28},{28,20},{20,12},{12,4},{4,0},{1,9},{9... | collective-permute-start | bytes 393224 | tf_op jit(solution)/shard_map/ppermute | solution.py:185
  64.6 11.4 %collective-permute-start.15 = (bf16[512,128]{1,0:T(8,128)(2,1)S(1)}, bf16[512,128]{1,0:T(8,128)(2,1)S(1)}, u32[]{:S(2)}, u32[]{:S(2)}) collective-permute-start(bf16[512,128]{1,0:T(8,128)(2,1)S(1)} %collective-permute-done.14.refs_4_), channel_id=1, source_target_pairs={{0,4},{8,0},{16,8},{24,16},{28,24},{20,28},{12,20},{4,12},{1,5},{9... | collective-permute-start | bytes 393224 | tf_op jit(solution)/shard_map/ppermute | solution.py:185
  65.0 16.0 %slice-start.4 = ((s8[16777216]{0:T(1024)(128)(4,1)}), s8[4194304]{0:T(1024)(128)(4,1)S(1)}, s32[]{:S(2)}) async-start(s8[16777216]{0:T(1024)(128)(4,1)} %bitcast.78), calls=%async_computation.4 | async-start | bytes 8388608
  65.0 16.0 %slice-start.5 = ((s8[16777216]{0:T(1024)(128)(4,1)}), s8[4194304]{0:T(1024)(128)(4,1)S(1)}, s32[]{:S(2)}) async-start(s8[16777216]{0:T(1024)(128)(4,1)} %bitcast.78), calls=%async_computation.5 | async-start | bytes 8388608
  68.9 5.0 %collective-permute-start.29 = (bf16[512,128]{1,0:T(8,128)(2,1)S(1)}, bf16[512,128]{1,0:T(8,128)(2,1)S(1)}, u32[]{:S(2)}, u32[]{:S(2)}) collective-permute-start(bf16[512,128]{1,0:T(8,128)(2,1)S(1)} %fusion.1.refs_0_), channel_id=1, source_target_pairs={{0,4},{8,0},{16,8},{24,16},{28,24},{20,28},{12,20},{4,12},{1,5},{9... | collective-permute-start | bytes 393224 | tf_op jit(solution)/shard_map/ppermute | solution.py:185
  69.3 5.4 %collective-permute-start.32 = (bf16[512,128]{1,0:T(8,128)(2,1)S(1)}, bf16[512,128]{1,0:T(8,128)(2,1)S(1)}, u32[]{:S(2)}, u32[]{:S(2)}) collective-permute-start(bf16[512,128]{1,0:T(8,128)(2,1)S(1)} %fusion.1.refs_0_), channel_id=1, source_target_pairs={{0,8},{8,16},{16,24},{24,28},{28,20},{20,12},{12,4},{4,0},{1,9},{9... | collective-permute-start | bytes 393224 | tf_op jit(solution)/shard_map/ppermute | solution.py:185
  71.0 5.0 %collective-permute-start.16 = (bf16[512,128]{1,0:T(8,128)(2,1)S(1)}, bf16[512,128]{1,0:T(8,128)(2,1)S(1)}, u32[]{:S(2)}, u32[]{:S(2)}) collective-permute-start(bf16[512,128]{1,0:T(8,128)(2,1)S(1)} %add_convert_fusion.1), channel_id=1, source_target_pairs={{0,8},{8,16},{16,24},{24,28},{28,20},{20,12},{12,4},{4,0},{1,9},{9... | collective-permute-start | bytes 393224 | tf_op jit(solution)/shard_map/ppermute | solution.py:185
  73.9 5.1 %collective-permute-start.30 = (bf16[512,128]{1,0:T(8,128)(2,1)S(1)}, bf16[512,128]{1,0:T(8,128)(2,1)S(1)}, u32[]{:S(2)}, u32[]{:S(2)}) collective-permute-start(bf16[512,128]{1,0:T(8,128)(2,1)S(1)} %collective-permute-done.29.refs_1_), channel_id=1, source_target_pairs={{0,4},{8,0},{16,8},{24,16},{28,24},{20,28},{12,20},{4,12},{1,5},{9... | collective-permute-start | bytes 393224 | tf_op jit(solution)/shard_map/ppermute | solution.py:185
  74.7 5.7 %collective-permute-start.33 = (bf16[512,128]{1,0:T(8,128)(2,1)S(1)}, bf16[512,128]{1,0:T(8,128)(2,1)S(1)}, u32[]{:S(2)}, u32[]{:S(2)}) collective-permute-start(bf16[512,128]{1,0:T(8,128)(2,1)S(1)} %collective-permute-done.32.refs_2_), channel_id=1, source_target_pairs={{0,8},{8,16},{16,24},{24,28},{28,20},{20,12},{12,4},{4,0},{1,9},{9... | collective-permute-start | bytes 393224 | tf_op jit(solution)/shard_map/ppermute | solution.py:185
  76.0 5.1 %slice-start.6 = ((s8[16777216]{0:T(1024)(128)(4,1)}), s8[4194304]{0:T(1024)(128)(4,1)S(1)}, s32[]{:S(2)}) async-start(s8[16777216]{0:T(1024)(128)(4,1)} %bitcast.78), calls=%async_computation.6 | async-start | bytes 8388608
  76.0 5.1 %slice-start.7 = ((s8[16777216]{0:T(1024)(128)(4,1)}), s8[4194304]{0:T(1024)(128)(4,1)S(1)}, s32[]{:S(2)}) async-start(s8[16777216]{0:T(1024)(128)(4,1)} %bitcast.78), calls=%async_computation.7 | async-start | bytes 8388608
  78.9 14.1 %collective-permute-start.17 = (f32[1024,128]{1,0:T(8,128)S(1)}, f32[1024,128]{1,0:T(8,128)S(1)}, u32[]{:S(2)}, u32[]{:S(2)}) collective-permute-start(f32[1024,128]{1,0:T(8,128)S(1)} %slice.92), channel_id=1, source_target_pairs={{0,1},{1,0},{2,3},{3,2},{4,5},{5,4},{6,7},{7,6},{8,9},{9,8},{10,11... | collective-permute-start | bytes 1572872 | tf_op jit(solution)/shard_map/ppermute | solution.py:188
  79.0 5.9 %collective-permute-start.31 = (bf16[512,128]{1,0:T(8,128)(2,1)S(1)}, bf16[512,128]{1,0:T(8,128)(2,1)S(1)}, u32[]{:S(2)}, u32[]{:S(2)}) collective-permute-start(bf16[512,128]{1,0:T(8,128)(2,1)S(1)} %collective-permute-done.30.refs_3_), channel_id=1, source_target_pairs={{0,4},{8,0},{16,8},{24,16},{28,24},{20,28},{12,20},{4,12},{1,5},{9... | collective-permute-start | bytes 393224 | tf_op jit(solution)/shard_map/ppermute | solution.py:185
  80.5 5.9 %collective-permute-start.34 = (bf16[512,128]{1,0:T(8,128)(2,1)S(1)}, bf16[512,128]{1,0:T(8,128)(2,1)S(1)}, u32[]{:S(2)}, u32[]{:S(2)}) collective-permute-start(bf16[512,128]{1,0:T(8,128)(2,1)S(1)} %collective-permute-done.33.refs_4_), channel_id=1, source_target_pairs={{0,8},{8,16},{16,24},{24,28},{28,20},{20,12},{12,4},{4,0},{1,9},{9... | collective-permute-start | bytes 393224 | tf_op jit(solution)/shard_map/ppermute | solution.py:185
  84.9 5.1 %collective-permute-start.35 = (bf16[512,128]{1,0:T(8,128)(2,1)S(1)}, bf16[512,128]{1,0:T(8,128)(2,1)S(1)}, u32[]{:S(2)}, u32[]{:S(2)}) collective-permute-start(bf16[512,128]{1,0:T(8,128)(2,1)S(1)} %add_convert_fusion), channel_id=1, source_target_pairs={{0,4},{8,0},{16,8},{24,16},{28,24},{20,28},{12,20},{4,12},{1,5},{9... | collective-permute-start | bytes 393224 | tf_op jit(solution)/shard_map/ppermute | solution.py:185
  92.9 2.0 %collective-permute-start.36 = (f32[1024,128]{1,0:T(8,128)S(1)}, f32[1024,128]{1,0:T(8,128)S(1)}, u32[]{:S(2)}, u32[]{:S(2)}) collective-permute-start(f32[1024,128]{1,0:T(8,128)S(1)} %slice.105), channel_id=1, source_target_pairs={{0,1},{1,0},{2,3},{3,2},{4,5},{5,4},{6,7},{7,6},{8,9},{9,8},{10,11... | collective-permute-start | bytes 1572872 | tf_op jit(solution)/shard_map/ppermute | solution.py:188
  93.1 9.2 %collective-permute-start.18 = (f32[512,128]{1,0:T(8,128)S(1)}, f32[512,128]{1,0:T(8,128)S(1)}, u32[]{:S(2)}, u32[]{:S(2)}) collective-permute-start(f32[512,128]{1,0:T(8,128)S(1)} %slice.117), channel_id=1, source_target_pairs={{0,2},{1,3},{2,0},{3,1},{4,6},{5,7},{6,4},{7,5},{8,10},{9,11},{10,... | collective-permute-start | bytes 786440 | tf_op jit(solution)/shard_map/ppermute | solution.py:188
  95.7 11.8 %collective-permute-start.37 = (f32[512,128]{1,0:T(8,128)S(1)}, f32[512,128]{1,0:T(8,128)S(1)}, u32[]{:S(2)}, u32[]{:S(2)}) collective-permute-start(f32[512,128]{1,0:T(8,128)S(1)} %get-tuple-element.29), channel_id=1, source_target_pairs={{0,2},{1,3},{2,0},{3,1},{4,6},{5,7},{6,4},{7,5},{8,10},{9,11},{10,... | collective-permute-start | bytes 786440 | tf_op jit(solution)/shard_map/ppermute | solution.py:188
  107.5 0.7 copy-start.2
